TPU v7x, 32 devices: a whole 2x2x4 slice. The times are simulated.
32 devices in a mesh: dp: 8 (over z, x), grp: 4 (over y, core).
Axes of the slice: x: 2, y: 2, z: 4, core: 2. Of those that a mesh axis runs over, the one named last changes fastest.
Arguments:
- inputs: bfloat16 [256, 128, 512], P(('dp', 'grp')), may hold values from -6 to 6
- top_down: bfloat16 [256, 128, 512], P(('dp', 'grp')), may hold values from -6 to 6
- lower_bounds: int32 [256, 128], P(('dp', 'grp')), may hold values 0 or 1
- h_init: float32 [256, 512], P(('dp', 'grp')), may hold values from -3 to 3
- c_init: float32 [256, 512], P(('dp', 'grp')), may hold values from -4 to 4
- z_init: float32 [256], P(('dp', 'grp')), may hold values from 0.1 to 0.9
- out_cot: bfloat16 [256, 128, 512], P(('dp', 'grp')), may hold values from -6 to 6
- gate_weight: float32 [1536, 2048], P('dp'), may hold values from -0.25 to 0.25
- gate_m: float32 [1536, 2048], P('dp'), may hold values from -4 to 4
- gate_v: float32 [1536, 2048], P('dp'), may hold values from 0.08192 to 0.32768
- small_params: float32 [5632], replicated, may hold values from -3 to 3
- small_m: float32 [5632], replicated, may hold values from -8.0453038 to 8.0453038
- small_v: float32 [5632], replicated, may hold values from 0.1605632 to 1.31072
Outputs:
- hidden_seq: bfloat16 [256, 128, 512], P(('dp', 'grp'))
- cell_last: float32 [256, 512], P(('dp', 'grp'))
- bounds_seq: float32 [256, 128], P(('dp', 'grp'))
- input_grad: float32 [256, 128, 512], P(('dp', 'grp'))
- weight_new: float32 [1536, 2048], P('dp')
- weight_m: float32 [1536, 2048], P('dp')
- weight_v: float32 [1536, 2048], P('dp')
- small_new: float32 [5632], replicated
- small_m_new: float32 [5632], replicated
- small_v_new: float32 [5632], replicated
All inputs are finite; a program needn't handle non-finite values. No bound on the sum of `lower_bounds` on one device may be relied on, other than what follows from the above.
Results may differ from a plain program's by a relative error of at most 0.0061.
Values may be sent and summed in bfloat16 or wider, within the bound.
No kernel may reach another device: no remote copies, remote signals or barrier semaphores. Data moves between devices by JAX's collectives and lax.ppermute only.
A program may use at most 192 MiB of HBM per device.

v0:
```python
import functools

import jax
import jax.numpy as jnp
from jax import lax
from jax.experimental import pallas as pl
from jax.experimental.pallas import tpu as pltpu
from jax.sharding import PartitionSpec as P

STEP = 10
TIME_BLOCK = 64
LANES = 128
VMEM_LIMIT = 60 * 1024 * 1024
CORE = 1
PLANE = 2
Z_SIZE = 4
BY_HAND = True
SMALL_VMEM = 16 * 1024 * 1024


beta_first = 0.9
beta_second = 0.999
epsilon = 1e-08
weight_rate = 0.05
small_rate = 0.1
decay_rate = 0.1

f32 = jnp.float32
bf16 = jnp.bfloat16


def adam_update(master, gradient, first_moment, second_moment, step_rate, weight_decay):
    m = beta_first * first_moment + (1.0 - beta_first) * gradient
    v = beta_second * second_moment + (1.0 - beta_second) * gradient * gradient
    m_hat = m / (1.0 - beta_first**STEP)
    v_hat = v / (1.0 - beta_second**STEP)
    updated = master - step_rate * (m_hat / (jnp.sqrt(v_hat) + epsilon) + weight_decay * master)
    return (updated, m, v)


def wide(column, count):
    return jnp.concatenate([column] * count, axis=1)


def lane_sum(array):
    return jnp.sum(array, axis=-1, keepdims=True)


def half_sigmoid(half):
    return 0.5 * jnp.tanh(half) + 0.5


def fold(array, units):
    parts = [array[:, at : at + units] for at in range(0, array.shape[1], units)]
    while len(parts) > 1:
        parts = [a + b for a, b in zip(parts[::2], parts[1::2])]
    return parts[0]


def lane_start(value):
    return pl.multiple_of(value, LANES)


def own_place():
    group, owner = lax.axis_index("grp"), lax.axis_index("dp")
    return lax.rem(group, 2), group // 2, lax.rem(owner, 2), owner // 2


def part_columns(place, width, side, chunk):
    core, plane = place[:2]
    core = core if side == 0 else 1 - core
    first = core * (width // 2) + chunk * (width // 4)
    small = width // 16
    offsets = (1 - plane, plane, 2 + plane, 3 - plane)
    return [lane_start(first + offset * small) for offset in offsets]


def weight_pieces(place, width, pieces):
    core, plane, x, z = place
    for index, (piece, blocks) in enumerate(pieces):
        if piece is None:
            yield index, 0, 0, 0
            continue
        far_core, far_plane, far_x, first = piece
        column = (1 - core if far_core else core) * (width // 2)
        column = column + (1 - plane if far_plane else plane) * (width // 4) + first
        for block in range(blocks):
            row = lax.rem(z - block + blocks, blocks) * 2 + (1 - x if far_x else x)
            yield index, block, row, lane_start(column)


TILE = 256
UNITS = 2


class Columns:
    def __init__(self, ref, first, rows):
        self.ref, self.first, self.shape = ref, first, (rows, ref.shape[0] * LANES)

    def tile(self, row, rows, column, lanes):
        row = self.first + row
        parts = [self.ref[at // LANES, row : row + rows, :] for at in range(column, column + lanes, LANES)]
        return jnp.concatenate(parts, axis=1)

    def all(self):
        return self.tile(0, self.shape[0], 0, self.shape[1])

    def store(self, row, column, value):
        for at in range(0, value.shape[1], LANES):
            rows = slice(self.first + row, self.first + row + value.shape[0])
            self.ref[(column + at) // LANES, rows, :] = value[:, at : at + LANES]


class ByHand:
    def __init__(self, weights, order, transpose, accumulators):
        self.weights, self.order, self.transpose = weights, order, transpose
        self.accumulators = accumulators

    def push(self, index):
        for unit in range(UNITS):
            rows, columns, _, _ = self.order[unit][index % len(self.order[unit])]
            tile = self.weights.tile(rows, TILE, columns, TILE)
            pltpu.matmul_push_rhs(tile, index % 2, unit, transpose=self.transpose)

    def begin(self, rows):
        self.push(0)
        self.push(1)
        self.load_first(rows)

    def load_first(self, rows):
        nothing = jnp.zeros((2 * rows, TILE), bf16)
        for unit in range(UNITS):
            pltpu.matmul_acc_lhs(self.accumulators[unit][0], nothing, load_staged_rhs=0)
        self.push(2)

    def multiply(self, left, index):
        for unit in range(UNITS):
            _, _, depth, column = self.order[unit][index]
            part = left[:, depth * TILE : (depth + 1) * TILE]
            staged = None if index == 0 else index % 2
            pltpu.matmul_acc_lhs(self.accumulators[unit][column], part, load_staged_rhs=staged)

    def pop(self, column):
        return [pltpu.matmul_pop(self.accumulators[unit][column]) for unit in range(UNITS)]

    def product(self, left):
        rows = left.shape[0]
        left = jnp.concatenate([left, jnp.zeros_like(left)], axis=0).astype(bf16)
        parts = []
        count = len(self.order[0])
        for index in range(count):
            self.multiply(left, index)
            if index > 0:
                self.push(index + 2)
            column = self.order[0][index][3]
            if index + 1 == count or self.order[0][index + 1][3] != column:
                parts += [part[:rows] for part in self.pop(column)]
        self.load_first(rows)
        return jnp.concatenate(parts, axis=1)

    def end(self, rows):
        left = jnp.zeros((2 * rows, TILE * (1 + max(entry[2] for entry in self.order[0]))), bf16)
        for index in range(3):
            self.multiply(left, index)
        for column in sorted({entry[3] for entry in self.order[0][:3]}):
            self.pop(column)


class ByCompiler:
    def __init__(self, weights, transpose):
        self.weights, self.transpose = weights, transpose

    def begin(self, rows):
        pass

    def product(self, left):
        dims = (((1,), (1 if self.transpose else 0,)), ((), ()))
        return lax.dot_general(left.astype(bf16), self.weights.all(), dims, preferred_element_type=f32)

    def end(self, rows):
        pass


def block_product(left_ref, weights, out):
    if not BY_HAND:
        out[...] = jnp.dot(left_ref[...], weights.all(), preferred_element_type=f32)
        return
    rows = left_ref.shape[0]
    depth, columns = weights.shape[0] // TILE, weights.shape[1] // TILE // UNITS
    count = depth * columns

    def body(accumulators):
        def tile(index, unit):
            return index % depth * TILE, (index // depth * UNITS + unit) * TILE

        def push(index):
            for unit in range(UNITS):
                row, column = tile(index, unit)
                part = weights.tile(row, TILE, column, TILE)
                pltpu.matmul_push_rhs(part, index % 2, unit)

        push(0)
        push(1)
        for index in range(count):
            for unit in range(UNITS):
                row, column = tile(index, unit)
                accumulator = accumulators[unit][index // depth % 2]
                pltpu.matmul_acc_lhs(accumulator, left_ref[:, row : row + TILE], load_staged_rhs=index % 2)
            if index + 2 < count:
                push(index + 2)
            if index % depth == depth - 1:
                for unit in range(UNITS):
                    row, column = tile(index, unit)
                    out[:, column : column + TILE] = pltpu.matmul_pop(accumulators[unit][index // depth % 2])

    pl.run_scoped(body, [[pltpu.ACC(unit)((rows, TILE), f32) for _ in range(2)] for unit in range(UNITS)])


def transpose(array, out):
    if not BY_HAND:
        out.store(0, 0, array.all().T)
        return
    high, columns = array.shape[0] // TILE // UNITS, array.shape[1] // TILE
    count = high * columns
    diagonal = lax.broadcasted_iota(jnp.int32, (TILE, TILE), 0) == lax.broadcasted_iota(
        jnp.int32, (TILE, TILE), 1
    )
    identity = jnp.where(diagonal, 1.0, 0.0).astype(bf16)

    def body(accumulators):
        def tile(index, unit):
            return (index // columns * UNITS + unit) * TILE, index % columns * TILE

        def push(index):
            for unit in range(UNITS):
                row, column = tile(index, unit)
                part = array.tile(row, TILE, column, TILE)
                pltpu.matmul_push_rhs(part, index % 2, unit, transpose=True)

        push(0)
        push(1)
        for index in range(count):
            for unit in range(UNITS):
                pltpu.matmul_acc_lhs(accumulators[unit][index % 2], identity, load_staged_rhs=index % 2)
            if index + 2 < count:
                push(index + 2)
            for unit in range(UNITS):
                row, column = tile(index, unit)
                part = pltpu.matmul_pop(accumulators[unit][index % 2])
                out.store(column, row, part.astype(bf16))

    pl.run_scoped(body, [[pltpu.ACC(unit)((TILE, TILE), f32) for _ in range(2)] for unit in range(UNITS)])


def matrix_product(body, weights, rows, transpose):
    if not BY_HAND:
        return body(ByCompiler(weights, transpose))
    high, wide_ = weights.shape
    depth, columns = (wide_ // TILE, high // TILE) if transpose else (high // TILE, wide_ // TILE)
    order = []
    for unit in range(UNITS):
        places = [(k, column) for column in range(columns // UNITS) for k in range(depth)]
        entries = []
        for k, column in places:
            at = (k * TILE, (column * UNITS + unit) * TILE)
            entries.append((*(at[::-1] if transpose else at), k, column))
        order.append(entries)
    shapes = [
        [pltpu.ACC(unit)((2 * rows, TILE), f32) for _ in range(columns // UNITS)] for unit in range(UNITS)
    ]
    return pl.run_scoped(
        lambda accumulators: body(ByHand(weights, order, transpose, accumulators)), shapes
    )


def sweep_kernel(
    rows,
    blocks,
    pieces,
    *refs,
):
    place = own_place()
    piece_refs, refs = refs[: len(pieces)], refs[len(pieces) :]
    (
        xb_ref,
        top_ref,
        cot_ref,
        bound_ref,
        z0_ref,
        h0_ref,
        c0_ref,
        small_ref,
        left_ref,
        hidden_ref,
        clast_ref,
        bounds_ref,
        w_parts_ref,
        own0_ref,
        own1_ref,
        other0_ref,
        other1_ref,
        dl_ref,
        gsmall_ref,
        w_ref,
        wt_s,
        xhat_s,
        gate_s,
        ftop_s,
        cell_s,
        tanh_s,
        hprev_s,
        bound_s,
        ds_s,
        zpre_s,
        zpost_s,
        rstd_s,
        rin_s,
        rtop_s,
        gain_s,
        gain_half_s,
        bias_half_s,
        vrec_s,
        wbar_s,
        sgain_s,
        sbias_s,
        svec_s,
        h_s,
        c_s,
        z_s,
        seq_s,
        in_sems,
        out_sems,
    ) = refs
    units = xb_ref.shape[1]
    width = w_ref.shape[0] * LANES
    tiles = units // LANES
    gate_tiles = width // LANES
    tokens = xb_ref.shape[0]
    pairs = tokens // (2 * rows)
    now = pl.program_id(0)
    forward = now < blocks
    block = jnp.where(forward, now, 2 * blocks - 1 - now)
    base = pl.multiple_of(block * tokens, tokens)
    part_refs = (own0_ref, own1_ref, other0_ref, other1_ref)
    part_blocks = [
        start // LANES for index in range(4) for start in part_columns(place, width, index // 2, index % 2)
    ]
    write_out = [
        pltpu.make_async_copy(
            w_ref.at[index, pl.ds(0, units), :], w_parts_ref.at[:, pl.ds(at * LANES, LANES)], out_sems.at[at]
        )
        for at, index in enumerate(part_blocks)
    ]

    lane = lax.broadcasted_iota(jnp.int32, (rows, LANES), 1)

    def vector(index):
        first = 2 * width + index * units
        return small_ref[:, first : first + units]

    @pl.when(now == 0)
    def _():
        copies = []
        for index, part, row, column in weight_pieces(place, width, pieces):
            ref = piece_refs[index]
            _, deep, lanes = ref.shape
            row = row * deep if isinstance(row, int) else pl.multiple_of(row * deep, deep)
            for at in range(lanes // LANES):
                source = ref.at[part, :, pl.ds(at * LANES, LANES)]
                into = w_ref.at[column // LANES + at, pl.ds(row, deep), :]
                copies.append(pltpu.make_async_copy(source, into, in_sems.at[len(copies)]))
        for copy in copies:
            copy.start()
        gain = jnp.broadcast_to(small_ref[:, :width], (rows, width))
        bias = jnp.broadcast_to(small_ref[:, width : 2 * width], (rows, width))
        split = 3 * units
        gain_s[...] = gain
        gain_half_s[:, :split] = (0.5 * width**0.5) * gain[:, :split]
        gain_half_s[:, split:] = width**0.5 * gain[:, split:]
        bias_half_s[:, :split] = 0.5 * bias[:, :split]
        bias_half_s[:, split:] = bias[:, split:]
        vrec_s[...] = jnp.broadcast_to(vector(1), (rows, units))
        h_s[...] = h0_ref[...]
        c_s[...] = c0_ref[...]
        row = lax.broadcasted_iota(jnp.int32, (rows, rows), 0)
        same = row == lax.broadcasted_iota(jnp.int32, (rows, rows), 1)
        z0 = jnp.where(same, jnp.broadcast_to(z0_ref[...], (rows, rows)), 0.0)
        z_s[...] = jnp.broadcast_to(lane_sum(z0), z_s.shape)
        seq_s[...] = jnp.zeros_like(seq_s)
        for copy in copies:
            copy.wait()
        for copy in write_out:
            copy.start()

        def row_means(matrix):
            matrix.begin(rows)
            wbar_s[...] = matrix.product(jnp.full((rows, width), 1.0 / width, f32))
            matrix.end(rows)

        matrix_product(row_means, Columns(w_ref, units, units), rows, True)

    def forward_step(matrix, local, h, c, z):
        at = pl.ds(pl.multiple_of(base + local, rows), rows)
        rec = matrix.product(h)
        low_f = h.astype(bf16).astype(f32)
        given = xhat_s[at, :] + wide(z, gate_tiles) * ftop_s[at, :]
        mean = lane_sum(low_f * wbar_s[...] + fold(given, units) * (1.0 / width))
        reach = lane_sum(low_f * vrec_s[...])
        b = bound_s[at, :]
        s = rec + (given - mean)
        squares = s * s
        parts = [fold(squares[:, at : at + units], LANES) for at in range(0, width, units)]
        root = lax.rsqrt(lane_sum(functools.reduce(jnp.add, parts)) + width * 1e-05)
        rstd = root * width**0.5
        half = (s * gain_half_s[...]) * root + bias_half_s[...]
        copied = (1.0 - z) * (1.0 - b)
        kept = (1.0 - z) * b
        fresh = wide(0.5 * (z + kept), tiles)
        half_c = wide(0.5 * kept, tiles) * c
        rest_c = half_c + wide(copied, tiles) * c
        gates = jnp.tanh(half)
        forget, inward, outward, candidate = (gates[:, k * units : (k + 1) * units] for k in range(4))
        c_next = (fresh * inward + fresh) * candidate + (forget * half_c + rest_c)
        th = jnp.tanh(c_next)
        forget, inward, outward = (0.5 * gate + 0.5 for gate in (forget, inward, outward))
        h_next = (wide(1.0 - copied, tiles) * outward) * th + wide(copied, tiles) * h
        z_next = half_sigmoid(0.5 * (rin_s[at, :] + reach + z * rtop_s[at, :]))
        xhat_s[at, :] = s * rstd
        gate_s[at, :units] = forget
        gate_s[at, units : 2 * units] = inward
        gate_s[at, 2 * units : 3 * units] = outward
        gate_s[at, 3 * units :] = candidate
        cell_s[at, :] = c
        tanh_s[at, :] = th
        hprev_s[at, :] = h
        zpre_s[at, :] = z
        zpost_s[at, :] = z_next
        rstd_s[at, :] = jnp.broadcast_to(rstd, z.shape)
        return h_next, c_next, z_next

    @pl.when(forward)
    def _():
        at = pl.ds(base, tokens)
        block_product(xb_ref, Columns(w_ref, 0, units), xhat_s.at[at, :])
        block_product(top_ref, Columns(w_ref, 2 * units, units), ftop_s.at[at, :])
        left_ref[:, :units] = xb_ref[...]
        shape = (tokens, LANES)
        rin_s[at, :] = jnp.broadcast_to(lane_sum(xb_ref[...].astype(f32) * vector(0)), shape)
        rtop_s[at, :] = jnp.broadcast_to(lane_sum(top_ref[...].astype(f32) * vector(2)), shape)
        for index in range(tokens // rows):
            column = lane_sum(jnp.where(lane == block * (tokens // rows) + index, bound_ref[...], 0.0))
            here = pl.ds(pl.multiple_of(base + index * rows, rows), rows)
            bound_s[here, :] = jnp.broadcast_to(column, (rows, LANES))

        def pair(matrix, index, carry):
            h0, c0, z0, seq = carry
            local = pl.multiple_of(index * 2 * rows, 2 * rows)
            h1, c1, z1 = forward_step(matrix, local, h0, c0, z0)
            h2, c2, z2 = forward_step(matrix, local + rows, h1, c1, z1)
            both = pl.ds(local, 2 * rows)
            left_ref[both, units : 2 * units] = jnp.concatenate([h0, h1], axis=0).astype(bf16)
            hidden_ref[both, :] = jnp.concatenate([h1, h2], axis=0).astype(bf16)
            z_pair = wide(jnp.concatenate([z0, z1], axis=0), tiles)
            left_ref[both, 2 * units :] = (top_ref[both, :].astype(f32) * z_pair).astype(bf16)
            step = block * (2 * pairs) + 2 * index
            seq = jnp.where(lane == step, z1, jnp.where(lane == step + 1, z2, seq))
            return h2, c2, z2, seq

        def steps(matrix):
            matrix.begin(rows)
            start = (h_s[...], c_s[...], z_s[...], seq_s[...])
            h, c, z, seq = lax.fori_loop(0, pairs, functools.partial(pair, matrix), start, unroll=4)
            matrix.end(rows)
            h_s[...] = h
            c_s[...] = c
            z_s[...] = z
            seq_s[...] = seq

        matrix_product(steps, Columns(w_ref, units, units), rows, False)

    @pl.when(now == blocks)
    def _():
        clast_ref[...] = c_s[...]
        bounds_ref[...] = seq_s[...]
        for copy in write_out:
            copy.wait()
        transpose(Columns(w_ref, units, units), Columns(wt_s, 0, width))
        h_s[...] = jnp.zeros_like(h_s)
        c_s[...] = jnp.zeros_like(c_s)
        z_s[...] = jnp.zeros_like(z_s)
        sgain_s[...] = jnp.zeros_like(sgain_s)
        sbias_s[...] = jnp.zeros_like(sbias_s)
        svec_s[...] = jnp.zeros_like(svec_s)

    def backward_step(matrix, local, cot, xb, top, bh_known, bh_mat, bc, bz):
        at = pl.ds(pl.multiple_of(base + local, rows), rows)
        z = zpre_s[at, :]
        b = bound_s[at, :]
        z_next = zpost_s[at, :]
        copied = (1.0 - z) * (1.0 - b)
        kept = (1.0 - z) * b
        fresh = z + kept
        c = cell_s[at, :]
        th = tanh_s[at, :]
        h = hprev_s[at, :]
        forget = gate_s[at, :units]
        inward = gate_s[at, units : 2 * units]
        outward = gate_s[at, 2 * units : 3 * units]
        candidate = gate_s[at, 3 * units :]
        xhat = xhat_s[at, :]
        rstd = rstd_s[at, :]
        new = wide(1.0 - copied, tiles) * outward
        written = inward * candidate
        by_dh = new * (1.0 - th * th)
        by_out = new * (th * (1.0 - outward))
        by_dc = (
            wide(kept, tiles) * c * (forget * (1.0 - forget)),
            wide(fresh, tiles) * (written * (1.0 - inward)),
            wide(fresh, tiles) * (inward * (1.0 - candidate * candidate)),
        )
        gain = [gain_s[:, k * units : (k + 1) * units] for k in range(4)]
        dh_known = bh_known + cot
        dh = dh_known + bh_mat
        dc = (bc + dh_known * by_dh) + bh_mat * by_dh
        d_out = dh * by_out
        dx_out = dh_known * (by_out * gain[2]) + bh_mat * (by_out * gain[2])
        dn = jnp.concatenate([dc * by_dc[0], dc * by_dc[1], d_out, dc * by_dc[2]], axis=1)
        dx = jnp.concatenate(
            [dc * (by_dc[0] * gain[0]), dc * (by_dc[1] * gain[1]), dx_out, dc * (by_dc[2] * gain[3])], axis=1
        )
        rstd_wide = wide(rstd, gate_tiles)
        sum1 = lane_sum(fold(dx, units))
        sum2 = lane_sum(fold(dx * xhat, units))
        ds = (rstd_wide * dx - (rstd_wide * (1.0 / width)) * sum1) - (xhat * rstd_wide * (1.0 / width)) * sum2
        bh_mat = matrix.product(ds)
        d_logit = bz * (z_next * (1.0 - z_next))
        bh_known = wide(copied, tiles) * dh + wide(d_logit, tiles) * vrec_s[...]
        bc_next = dc * (wide(kept, tiles) * forget + wide(copied, tiles))
        by_z = dc * (written - wide(b, tiles) * (forget * c + written) - wide(1.0 - b, tiles) * c)
        by_z = by_z - wide(1.0 - b, tiles) * (dh * (h - outward * th))
        bz_next = lane_sum(fold(ds * ftop_s[at, :], units) + by_z) + d_logit * rtop_s[at, :]
        sgain_s[...] += dn * xhat
        sbias_s[...] += dn
        low = h.astype(bf16).astype(f32)
        svec_s[:, :units] += wide(d_logit, tiles) * xb
        svec_s[:, units : 2 * units] += wide(d_logit, tiles) * low
        svec_s[:, 2 * units :] += wide(d_logit * z, tiles) * top
        return ds, d_logit, (bh_known, bh_mat, bc_next, bz_next)

    @pl.when(jnp.logical_not(forward))
    def _():
        def pair(matrix, index, carry):
            local = pl.multiple_of((pairs - 1 - index) * 2 * rows, 2 * rows)
            both = pl.ds(local, 2 * rows)
            given = [ref[both, :].astype(f32) for ref in (cot_ref, xb_ref, top_ref)]
            seq, *carry = carry
            ds1, dl1, carry = backward_step(matrix, local + rows, *(array[rows:] for array in given), *carry)
            ds0, dl0, carry = backward_step(matrix, local, *(array[:rows] for array in given), *carry)
            ds = jnp.concatenate([ds0, ds1], axis=0).astype(bf16)
            for at in range(gate_tiles):
                ds_s[at, :, :] = ds[:, at * LANES : (at + 1) * LANES]
            for at, index in enumerate(part_blocks):
                part_refs[at // tiles][both, at % tiles * LANES : (at % tiles + 1) * LANES] = ds_s[index, :, :]
            step = (base + local) // rows
            seq = jnp.where(lane == step, dl0, jnp.where(lane == step + 1, dl1, seq))
            return (seq, *carry)

        def steps(matrix):
            matrix.begin(rows)
            start = (seq_s[...], h_s[...], jnp.zeros((rows, units), f32), c_s[...], z_s[...])
            seq, bh_known, bh_mat, bc, bz = lax.fori_loop(0, pairs, functools.partial(pair, matrix), start, unroll=4)
            matrix.end(rows)
            h_s[...] = bh_known + bh_mat
            c_s[...] = bc
            z_s[...] = bz
            seq_s[...] = seq

        matrix_product(steps, Columns(wt_s, 0, width), rows, False)

    @pl.when(now == 2 * blocks - 1)
    def _():
        dl_ref[...] = seq_s[...]
        gsmall_ref[...] = jnp.zeros_like(gsmall_ref)
        row = 0
        for ref in (sgain_s, sbias_s, svec_s):
            total = jnp.sum(ref[...], axis=0, keepdims=True)
            for at in range(0, total.shape[1], LANES):
                gsmall_ref[row : row + 1, :] = total[:, at : at + LANES]
                row += 1


def sweep(described, pieces, xb, top, cot, bounds, z0, h0, c0, small_params):
    tokens, units = xb.shape
    rows = h0.shape[0]
    width = 4 * units
    block = TIME_BLOCK * rows
    blocks = tokens // block
    small_rows = -(-small_params.shape[1] // (16 * LANES)) * 16

    def both_ways(lanes):
        return pl.BlockSpec((block, lanes), lambda i: (jnp.where(i < blocks, i, 2 * blocks - 1 - i), 0))

    def going(lanes):
        return pl.BlockSpec((block, lanes), lambda i: (jnp.minimum(i, blocks - 1), 0))

    def returning(lanes):
        return pl.BlockSpec((block, lanes), lambda i: (jnp.minimum(blocks - 1, 2 * blocks - 1 - i), 0))

    def whole(shape):
        return pl.BlockSpec(shape, lambda i: (0, 0))

    anywhere = pl.BlockSpec(memory_space=pl.ANY)
    outs = [
        (going(3 * units), (tokens, 3 * units), bf16),
        (going(units), (tokens, units), bf16),
        (whole((rows, units)), (rows, units), f32),
        (whole((rows, LANES)), (rows, LANES), f32),
        (anywhere, (units, width), bf16),
        *[(returning(units), (tokens, units), bf16)] * 4,
        (whole((rows, LANES)), (rows, LANES), f32),
        (whole((small_rows, LANES)), (small_rows, LANES), f32),
    ]
    constants = (bounds, z0, h0, c0, small_params)
    return pl.pallas_call(
        functools.partial(sweep_kernel, rows, blocks, described),
        grid=(2 * blocks,),
        in_specs=[anywhere] * len(pieces)
        + [both_ways(units), both_ways(units), returning(units)]
        + [whole(array.shape) for array in constants],
        out_specs=[spec for spec, _, _ in outs],
        out_shape=[jax.ShapeDtypeStruct(shape, dtype) for _, shape, dtype in outs],
        scratch_shapes=[
            pltpu.VMEM((width // LANES, 3 * units, LANES), bf16),
            pltpu.VMEM((units // LANES, width, LANES), bf16),
            *[pltpu.VMEM((tokens, width), f32)] * 3,
            *[pltpu.VMEM((tokens, units), f32)] * 3,
            pltpu.VMEM((tokens, LANES), f32),
            pltpu.VMEM((width // LANES, 2 * rows, LANES), bf16),
            *[pltpu.VMEM((tokens, LANES), f32)] * 5,
            *[pltpu.VMEM((rows, width), f32)] * 3,
            *[pltpu.VMEM((rows, units), f32)] * 2,
            *[pltpu.VMEM((rows, width), f32)] * 2,
            pltpu.VMEM((rows, 3 * units), f32),
            *[pltpu.VMEM((rows, units), f32)] * 2,
            *[pltpu.VMEM((rows, LANES), f32)] * 2,
            pltpu.SemaphoreType.DMA((sum(piece.shape[0] * piece.shape[2] // LANES for piece in pieces),)),
            pltpu.SemaphoreType.DMA((width // LANES,)),
        ],
        compiler_params=pltpu.CompilerParams(
            dimension_semantics=("arbitrary",), vmem_limit_bytes=VMEM_LIMIT
        ),
        cost_estimate=pl.CostEstimate(flops=130 * 10**9, bytes_accessed=10**8, transcendentals=0),
        name="sweep",
    )(*pieces, xb, top, cot, *constants)


def adam_kernel(chunk, *refs):
    grads, (w_ref, m_ref, v_ref), (*outs, new_s, sems) = refs[:4], refs[4:7], refs[-5:]
    core, plane, _, _ = own_place()
    quarter = w_ref.shape[1] // 4
    copies = []
    for side in range(2):
        start = (1 - core if side else core) * (2 * quarter) + chunk * quarter
        for far_plane in range(2):
            grad_ref = grads[2 * side + far_plane]
            lanes = grad_ref.shape[1] // 2
            for half in range(2):
                at = (2 * half + (1 - plane if far_plane else plane)) * lanes
                columns = pl.ds(lane_start(start + at), lanes)
                grad = grad_ref[:, half * lanes : (half + 1) * lanes].astype(f32)
                new = adam_update(
                    w_ref[:, columns], grad, m_ref[:, columns], v_ref[:, columns], weight_rate, decay_rate
                )
                for index, value in enumerate(new):
                    new_s[index, side, :, pl.ds(lane_start(at), lanes)] = value
        for index, ref in enumerate(outs):
            into = ref.at[:, pl.ds(lane_start(start), quarter)]
            copies.append(pltpu.make_async_copy(new_s.at[index, side], into, sems.at[index, side]))
            copies[-1].start()
    for copy in copies:
        copy.wait()


def adam_columns(chunk, grads, master, first_moment, second_moment, earlier):
    rows, width = master.shape
    in_vmem, anywhere = pl.BlockSpec(memory_space=pltpu.VMEM), pl.BlockSpec(memory_space=pl.ANY)
    return pl.pallas_call(
        functools.partial(adam_kernel, chunk),
        in_specs=[in_vmem] * 7 + [anywhere] * len(earlier),
        out_specs=[anywhere] * 3,
        out_shape=[jax.ShapeDtypeStruct(master.shape, f32)] * 3,
        scratch_shapes=[pltpu.VMEM((3, 2, rows, width // 4), f32), pltpu.SemaphoreType.DMA((3, 2))],
        input_output_aliases={7 + k: k for k in range(len(earlier))},
        compiler_params=pltpu.CompilerParams(vmem_limit_bytes=SMALL_VMEM),
        name="adam",
    )(*grads, master, first_moment, second_moment, *earlier)


def after(value, others):
    return lax.optimization_barrier((value, others))[0]


def swap(array, bit, axis="grp"):
    count = lax.axis_size(axis)
    return lax.ppermute(array, axis, [(index, index ^ bit) for index in range(count)])


def along_z(array, step):
    count = lax.axis_size("dp")
    return lax.ppermute(array, "dp", [(index, (index + 2 * step) % count) for index in range(count)])


def gather_weights(shard, core, plane, ready):
    width = shard.shape[1]
    count = lax.axis_size("dp")
    if count != Z_SIZE * 2:
        return (None,), (lax.all_gather(shard.astype(bf16), "dp", axis=0, tiled=True)[None],)
    quarter = width // 4
    lanes = quarter // 2
    half = lanes // 2
    firsts = (0, lanes)
    owns = [
        lax.dynamic_slice_in_dim(
            shard, core * (width // 2) + plane * quarter + first, lanes, axis=1
        ).astype(bf16)
        for first in firsts
    ]

    def line(own):
        return tuple(along_z(own, step) for step in range(1, Z_SIZE))

    def planes(own, arrived):
        mine = jnp.stack((own,) + arrived)
        return mine, swap(mine, 1, "dp"), swap(mine, PLANE)

    def corners(pieces):
        return pieces[1][..., :half], pieces[2][..., half:]

    def corner_swap(from_x, from_y):
        return swap(from_x, PLANE), swap(from_y, 1, "dp")

    arrived0 = line(owns[0])
    own1 = after(owns[1], arrived0)
    arrived1 = line(own1)
    pieces0 = planes(owns[0], after(arrived0, ready))
    corners0 = corners(pieces0)
    pieces1 = planes(own1, after(arrived1, corners0))
    corners1 = corners(pieces1)
    all_pieces = [pieces0 + corner_swap(*corners0), pieces1 + corner_swap(*corners1)]
    kinds, pieces = [], []
    for first, here in zip(firsts, all_pieces):
        for far_core in (False, True):
            kinds += [
                (far_core, False, False, first),
                (far_core, False, True, first),
                (far_core, True, False, first),
                (far_core, True, True, first),
                (far_core, True, True, first + half),
            ]
            pieces += [swap(piece, CORE) for piece in after(here, corners1)] if far_core else here
    return tuple(kinds), tuple(pieces)


def split(value):
    high = value.astype(bf16)
    return high, (value - high.astype(f32)).astype(bf16)


def joined(high, low):
    return high.astype(f32) + low.astype(f32)


def both_parts(value):
    return joined(*split(value))


def small_call(kernel, arrays, extra, outs, extra_out=False):
    arrays = [*arrays, *extra]
    if extra_out:
        outs = outs + [(array.shape, array.dtype) for array in extra]
    return pl.pallas_call(
        functools.partial(kernel, len(extra)),
        in_specs=[pl.BlockSpec(memory_space=pltpu.VMEM)] * len(arrays),
        out_specs=[pl.BlockSpec(memory_space=pltpu.VMEM)] * len(outs),
        out_shape=[jax.ShapeDtypeStruct(shape, dtype) for shape, dtype in outs],
        compiler_params=pltpu.CompilerParams(vmem_limit_bytes=SMALL_VMEM),
        name=kernel.__name__,
    )(*arrays)


def first_kernel(with_small, total_ref, *refs):
    small_refs, (to_y_ref, to_x_ref) = refs[:with_small], refs[with_small:]
    _, _, x, _ = own_place()
    _, _, rows, columns = total_ref.shape
    small = columns // 4
    for index in range(2 * Z_SIZE):
        to_y_ref[index * rows : (index + 1) * rows, :] = total_ref[index // 2, index % 2, :, :small].astype(bf16)
    if with_small:
        deep = small_refs[0].shape[0]
        start = 2 * Z_SIZE * rows
        high, low = split(small_refs[0][...])
        to_y_ref[start : start + deep, :] = high
        to_y_ref[start + deep :, :] = low
    to_x_ref[...] = total_ref[:, 1 - x, :, 2 * small :].astype(bf16)


def second_kernel(with_small, total_ref, from_y_ref, from_x_ref, *refs):
    small_refs, (to_x_ref, to_y_ref, kept_ref, *small_outs) = refs[:with_small], refs[with_small:]
    _, _, x, _ = own_place()
    _, _, rows, columns = total_ref.shape
    small = columns // 4
    middle = slice(small, 2 * small)

    def from_y(index, of_x):
        start = (2 * index + of_x) * rows
        if rows % 16 == 0:
            start = pl.multiple_of(start, 16)
        return from_y_ref[pl.ds(start, rows), :].astype(f32)

    for index in range(Z_SIZE):
        away = total_ref[index, 1 - x, :, middle] + from_y(index, 1 - x)
        to_x_ref[index * rows : (index + 1) * rows, :] = away.astype(bf16)
        kept_ref[index, :, :small] = total_ref[index, x, :, middle] + from_y(index, x)
    right = total_ref[:, x, :, 2 * small :] + from_x_ref[...].astype(f32)
    kept_ref[..., small:] = right[..., :small]
    to_y_ref[...] = right[..., small:].astype(bf16)
    if with_small:
        deep = small_refs[0].shape[0]
        start = 2 * Z_SIZE * rows
        arrived = joined(from_y_ref[start : start + deep, :], from_y_ref[start + deep :, :])
        value = both_parts(small_refs[0][...]) + arrived
        small_outs[0][...] = value
        start = Z_SIZE * rows
        high, low = split(value)
        to_x_ref[start : start + deep, :] = high
        to_x_ref[start + deep :, :] = low


def third_kernel(with_small, kept_ref, from_x_ref, from_y_ref, *refs):
    small_refs, (own_ref, *away_refs) = refs[:with_small], refs[with_small:]
    _, _, _, z = own_place()
    _, rows, columns = kept_ref.shape
    small = columns // 2
    small_outs, away_refs = away_refs[Z_SIZE - 1 :], away_refs[: Z_SIZE - 1]
    for step, ref in enumerate([own_ref] + away_refs):
        at = lax.rem(z + step, Z_SIZE)
        start = at * rows
        if rows % 16 == 0:
            start = pl.multiple_of(start, 16)
        left = kept_ref[at, :, :small] + from_x_ref[pl.ds(start, rows), :].astype(f32)
        ref[:rows, :small] = left.astype(ref.dtype)
        ref[:rows, small:] = (kept_ref[at, :, small:] + from_y_ref[at].astype(f32)).astype(ref.dtype)
    if with_small:
        deep = small_refs[0].shape[0]
        start = Z_SIZE * rows
        arrived = joined(from_x_ref[start : start + deep, :], from_x_ref[start + deep :, :])
        value = both_parts(small_refs[0][...]) + arrived
        small_outs[0][...] = value
        high, low = split(value)
        for ref in away_refs:
            ref[rows:, :small] = high
            ref[rows:, small:] = low


def fourth_kernel(with_small, own_ref, *refs):
    arrived, refs = refs[: Z_SIZE - 1], refs[Z_SIZE - 1 :]
    small_refs, (out_ref, *small_outs) = refs[:with_small], refs[with_small:]
    rows, columns = own_ref.shape
    small = columns // 2
    total = own_ref[...]
    for ref in arrived:
        total = total + ref[:rows, :].astype(f32)
    out_ref[...] = total.astype(bf16)
    if with_small:
        one, two, three = (joined(ref[rows:, :small], ref[rows:, small:]) for ref in arrived)
        value = (both_parts(small_refs[0][...]) + two) + (one + three)
        small_outs[0][:, :small], small_outs[0][:, small:] = split(value)


def reduce_rows(totals, grad_small, late, late_inputs):
    count = lax.axis_size("dp")
    all_rows, columns = totals[0].shape
    small = columns // 4
    deep = grad_small.shape[0]
    if count != Z_SIZE * 2:
        sums = []
        for total in totals:
            mine = lax.psum_scatter(total.astype(bf16), "dp", scatter_dimension=0, tiled=True).astype(f32)
            away = jnp.concatenate([mine[:, :small], mine[:, 3 * small :]], axis=1).astype(bf16)
            sums.append((mine[:, small : 3 * small] + swap(away, PLANE).astype(f32)).astype(bf16))
        total = grad_small + swap(grad_small, PLANE)
        bit = 1
        while bit < count:
            total = total + swap(total, bit, "dp")
            bit *= 2
        return sums, jnp.concatenate(split(total), axis=1), late(*late_inputs)
    rows = all_rows // count
    totals = [total.reshape(Z_SIZE, 2, rows, columns) for total in totals]

    def first(total, extra):
        below = 2 * deep if extra else 0
        outs = [((2 * Z_SIZE * rows + below, small), bf16), ((Z_SIZE, rows, 2 * small), bf16)]
        return small_call(first_kernel, [total], extra, outs)

    def first_swap(to_y, to_x):
        return swap(to_y, PLANE), swap(to_x, 1, "dp")

    def second(total, arrived, extra):
        below = 2 * deep if extra else 0
        outs = [
            ((Z_SIZE * rows + below, small), bf16),
            ((Z_SIZE, rows, small), bf16),
            ((Z_SIZE, rows, 2 * small), f32),
        ]
        return small_call(second_kernel, [total, *arrived], extra, outs, True)

    def second_swap(to_x, to_y, kept):
        return kept, swap(to_x, 1, "dp"), swap(to_y, PLANE)

    def third(arrived, extra):
        below = deep if extra else 0
        outs = [((rows, 2 * small), f32)] + [((rows + below, 2 * small), bf16)] * (Z_SIZE - 1)
        return small_call(third_kernel, arrived, extra, outs, True)

    def third_swap(own, *away):
        return (own,) + tuple(along_z(array, step + 1) for step, array in enumerate(away))

    def fourth(arrived, extra):
        outs = [((rows, 2 * small), bf16)] + [((deep, 2 * small), bf16)] * len(extra)
        return small_call(fourth_kernel, arrived, extra, outs)

    extra = [grad_small]
    out0 = first(totals[0], extra)
    in0 = first_swap(*out0)
    out1 = first(totals[1], [])
    in1 = first_swap(*out1)
    *out0, value = second(totals[0], in0, extra)
    extra = [value]
    in0 = second_swap(*out0)
    out1 = second(totals[1], after(in1, out0), [])
    in1 = second_swap(*out1)
    *out0, value = third(after(in0, out1), extra)
    extra = [value]
    in0 = third_swap(*out0)
    out1 = third(after(in1, out0), [])
    late_outputs = late(*after(late_inputs, out1))
    in1 = third_swap(*out1)
    sum0, small_pair = fourth(after(in0, (late_outputs, in1[1])), extra)
    (sum1,) = fourth(after(in1, sum0), [])
    return [sum0, sum1], small_pair, late_outputs


def shards(
    inputs,
    top_down,
    lower_bounds,
    h_init,
    c_init,
    z_init,
    out_cot,
    gate_weight,
    gate_m,
    gate_v,
    small_params,
    small_m,
    small_v,
):
    rows, steps, units = inputs.shape
    tokens = rows * steps
    width = 4 * units
    core, plane, _, _ = own_place()

    def by_time(array):
        return jnp.swapaxes(array, 0, 1).reshape((tokens,) + array.shape[2:])

    def by_window(array):
        return jnp.swapaxes(array.reshape((steps, rows) + array.shape[1:]), 0, 1)

    bound = by_time(lower_bounds).astype(f32)
    ready = (
        by_time(inputs) * bound[:, None].astype(bf16),
        by_time(top_down),
        by_time(out_cot),
        jnp.pad(lower_bounds.astype(f32), ((0, 0), (0, LANES - steps))),
        z_init[None],
        small_params[None],
    )
    kinds, pieces = gather_weights(gate_weight, core, plane, ready)
    described = tuple((kind, piece.shape[0]) for kind, piece in zip(kinds, pieces))
    xb, top, cot, bounds_f, z0, small_row = ready
    left, hidden, c_last, bounds, w_parts, own0, own1, other0, other1, d_logit, grad_small = sweep(
        described, pieces, xb, top, cot, bounds_f, z0, h_init, c_init, small_row
    )

    def product(right):
        return lax.dot_general(left, right, (((0,), (0,)), ((), ())), preferred_element_type=f32)

    totals = []
    for own, other in ((own0, other0), (own1, other1)):
        from_core = swap(product(other).astype(bf16), CORE)
        totals.append(product(own) + from_core.astype(f32))
    v_input = small_params[2 * width : 2 * width + units]

    def late(d_logit, hidden, *parts):
        by_input = 0.0
        for index, part in enumerate(parts):
            columns = w_parts[:, index * units : (index + 1) * units]
            by_input = by_input + lax.dot_general(
                part, columns, (((1,), (1,)), ((), ())), preferred_element_type=f32
            )
        by_logit = lower_bounds.astype(f32) * d_logit[:, :steps]
        input_grad = by_window(bound[:, None] * by_input) + by_logit[:, :, None] * v_input
        return by_window(hidden), input_grad

    late_inputs = d_logit, hidden, own0, own1, other0, other1
    sums, small_pair, (hidden, input_grad) = reduce_rows(totals, grad_small, late, late_inputs)
    weights = ()
    for chunk, grad in enumerate(sums):
        far = swap(grad, PLANE)
        grads = [grad, far, swap(after(grad, far), CORE), swap(grad, CORE | PLANE)]
        if chunk == 0:
            near_pair = swap(after(small_pair, far), CORE)
        weights = adam_columns(chunk, grads, gate_weight, gate_m, gate_v, weights)
    weight_new, weight_m, weight_v = weights
    small_total = 0.0
    for pair in (small_pair, near_pair):
        small_total = small_total + joined(pair[:, :LANES], pair[:, LANES:])
    small_total = small_total.reshape(-1)[: small_params.shape[0]]

    small_new, small_m_new, small_v_new = adam_update(
        small_params, small_total, small_m, small_v, small_rate, 0.0
    )
    return (
        hidden,
        c_last,
        bounds[:, :steps],
        input_grad,
        weight_new,
        weight_m,
        weight_v,
        small_new,
        small_m_new,
        small_v_new,
    )


def solution(mesh):
    def program(*arrays):
        with jax.sharding.use_abstract_mesh(mesh.abstract_mesh):
            return sharded(*arrays)

    tokens = P(("dp", "grp"), None, None)
    windows = P(("dp", "grp"), None)
    owned = P("dp", None)
    in_specs = (
        (tokens, tokens, windows, windows, windows, P(("dp", "grp")), tokens)
        + (owned,) * 3
        + (P(),) * 3
    )
    out_specs = (tokens, windows, windows, tokens) + (owned,) * 3 + (P(),) * 3
    sharded = jax.shard_map(shards, mesh=mesh, in_specs=in_specs, out_specs=out_specs, check_vma=False)
    return program
```

profile of v0, /device:TPU:17, one launch (start us, length us, event | category | flops | bytes accessed | tf_op | source)
XLA Modules:
  0.0 243.3 jit_solution(5406863576628671194)
XLA Ops:
  0.7 1.1 dynamic-slice_convert_fusion
  1.7 1.3 collective-permute-start
  3.1 1.2 collective-permute-start.2
  4.3 1.3 fusion.16
  5.8 4.1 %copy_bitcast_fusion.1 = (bf16[1024,512]{1,0:T(8,128)(2,1)}, bf16[1024,512]{1,0:T(8,128)(2,1)}) fusion(bf16[128,8,512]{2,0,1:T(8,128)(2,1)} %bitcast.56, bf16[128,8,512]{2,0,1:T(8,128)(2,1)} %bitcast.57), kind=kLoop, calls=%fused_computation.8 | loop fusion | bytes 4194304 | tf_op jit(solution)/shard_map/reshape | solution.py:974
  9.9 1.6 bitcast_multiply_fusion.refs_20_
  11.5 0.6 broadcast_in_dim.5.refs_27_
  12.2 1.3 collective-permute-start.3
  13.5 1.2 collective-permute-start.4
  14.7 0.6 collective-permute-start.7
  15.3 2.3 collective-permute-start.8
  17.6 1.6 collective-permute-start.9
  19.3 2.4 collective-permute-done.3.refs_1_
  21.7 0.7 collective-permute-done.4.refs_2_
  22.5 1.4 collective-permute-done.8
  23.9 2.2 collective-permute-done.9
  26.7 1.2 collective-permute-start.5
  28.0 1.2 collective-permute-start.6
  29.2 6.8 %collective-permute-done.10.refs_11_ = bf16[4,192,256]{2,1,0:T(8,128)(2,1)S(1)} collective-permute-done((bf16[4,192,256]{2,1,0:T(8,128)(2,1)S(1)}, bf16[4,192,256]{2,1,0:T(8,128)(2,1)S(1)}, u32[]{:S(2)}, u32[]{:S(2)}) %collective-permute-start.10) | collective-permute-done | bytes 393248 | tf_op jit(solution)/shard_map/ppermute | solution.py:705
  36.4 0.9 collective-permute-start.18
  37.3 2.9 %collective-permute-done.5.refs_3_ = bf16[4,192,128]{2,1,0:T(8,128)(2,1)S(1)} collective-permute-done((bf16[4,192,128]{2,1,0:T(8,128)(2,1)S(1)}, bf16[4,192,128]{2,1,0:T(8,128)(2,1)S(1)}, u32[]{:S(2)}, u32[]{:S(2)}) %collective-permute-start.5) | collective-permute-done | bytes 196640 | tf_op jit(solution)/shard_map/ppermute | solution.py:705
  40.2 3.7 %collective-permute-start.12 = (bf16[4,192,256]{2,1,0:T(8,128)(2,1)S(1)}, bf16[4,192,256]{2,1,0:T(8,128)(2,1)S(1)}, u32[]{:S(2)}, u32[]{:S(2)}) collective-permute-start(bf16[4,192,256]{2,1,0:T(8,128)(2,1)S(1)} %pad_maximum_fusion.refs_0_), channel_id=1, source_target_pairs={{0,1},{1,0},{2,3},{3,2},{4,5},{5,4},{6,7},{7,6},{8,9},{9,8},{10,11... | collective-permute-start | bytes 1179656 | tf_op jit(solution)/shard_map/ppermute | solution.py:705
  44.5 2.0 collective-permute-start.22
  48.6 0.5 collective-permute-done.14.refs_7_
  49.1 0.6 collective-permute-done.19.refs_15_
  49.7 1.1 collective-permute-done.20.refs_16_
  50.8 0.8 copy-done.29
  51.7 120.0 %sweep.1 = (bf16[1024,1536]{1,0:T(8,128)(2,1)}, bf16[1024,512]{1,0:T(8,128)(2,1)}, f32[8,512]{1,0:T(8,128)}, f32[8,128]{1,0:T(8,128)}, bf16[512,2048]{1,0:T(8,12...) custom-call(bf16[4,192,256]{2,1,0:T(8,128)(2,1)} %copy-done.11, ...), custom_call_target="tpu_custom_call" | custom-call | flops 130000003072 | bytes 100000000 | tf_op jit(solution)/shard_map/sweep/pallas_call | solution.py:624
  171.7 4.2 %convolution_convert_fusion = bf16[1536,512]{1,0:T(8,128)(2,1)S(1)} fusion(bf16[1024,1536]{1,0:T(8,128)(2,1)} %get-tuple-element.114, bf16[1024,512]{1,0:T(8,128)(2,1)} %get-tuple-element.149), kind=kOutput, calls=%fused_computation.2 | convolution fusion | flops 1611399168 | bytes 5767168 | tf_op jit(solution)/shard_map/dot_general | solution.py:996
  176.3 1.8 convolution_convert_fusion.1
  178.4 1.0 collective-permute-done.27
  179.4 1.9 convolution_add_fusion
  181.8 1.2 collective-permute-start.29
  183.0 1.9 convolution_add_fusion.1
  185.0 1.2 collective-permute-start.25
  186.5 5.5 %collective-permute-done.29.from_x_ref = bf16[4,192,256]{2,1,0:T(8,128)(2,1)S(1)} collective-permute-done((bf16[4,192,256]{2,1,0:T(8,128)(2,1)S(1)}, bf16[4,192,256]{2,1,0:T(8,128)(2,1)S(1)}, u32[]{:S(2)}, u32[]{:S(2)}) %collective-permute-start.29) | collective-permute-done | bytes 393248 | tf_op jit(solution)/shard_map/ppermute | solution.py:705
  192.7 1.3 collective-permute-start.32
  194.0 0.6 collective-permute-start.33
  194.6 6.3 %collective-permute-done.25.from_y_ref = bf16[1536,128]{1,0:T(8,128)(2,1)S(1)} collective-permute-done((bf16[1536,128]{1,0:T(8,128)(2,1)S(1)}, bf16[1536,128]{1,0:T(8,128)(2,1)S(1)}, u32[]{:S(2)}, u32[]{:S(2)}) %collective-permute-start.25) | collective-permute-done | bytes 393248 | tf_op jit(solution)/shard_map/ppermute | solution.py:705
  201.1 1.3 collective-permute-start.30
  202.4 0.6 collective-permute-start.31
  203.0 2.1 collective-permute-done.33.from_y_ref
  205.3 1.9 collective-permute-start.37
  207.2 1.5 collective-permute-start.38
  209.5 2.2 collective-permute-start.34
  211.7 1.5 collective-permute-start.35
  213.2 0.7 fusion.6
  213.9 0.7 fusion.8
  215.2 0.7 fusion.4
  216.0 0.8 multiply_bitcast_fusion
  216.8 2.6 %bitcast_add_fusion = f32[8,128,512]{2,1,0:T(8,128)} fusion(f32[128,8,512]{2,1,0:T(8,128)S(1)} %multiply_bitcast_fusion, f32[512]{0:T(512)S(1)} %slice-done, f32[8,128]{1,0:T(8,128)S(1)} %convert_multiply_fusion), kind=kLoop, calls=%fused_computation.4 | loop fusion | flops 1048576 | bytes 4200448 | tf_op jit(solution)/shard_map/add | solution.py:1012
  219.4 1.3 copy.42
  221.1 1.0 collective-permute-done.39.refs_2_
  222.5 1.7 collective-permute-done.35.refs_1_
  224.2 1.9 collective-permute-done.36.refs_2_
  226.2 0.5 collective-permute-start.40
  226.7 5.4 %collective-permute-start.46 = (bf16[48,256]{1,0:T(8,128)(2,1)S(1)}, bf16[48,256]{1,0:T(8,128)(2,1)S(1)}, u32[]{:S(2)}, u32[]{:S(2)}) collective-permute-start(bf16[48,256]{1,0:T(8,128)(2,1)S(1)} %get-tuple-element.171), channel_id=1, source_target_pairs={{0,1},{1,0},{2,3},{3,2},{4,5},{5,4},{6,7},{7,6},{8,9},{9,8},{10,11... | collective-permute-start | bytes 73736 | tf_op jit(solution)/shard_map/ppermute | solution.py:705
  232.1 0.7 collective-permute-start.45
  232.8 1.1 collective-permute-start.42
  233.9 2.4 collective-permute-start.41
  236.3 0.6 multiply_subtract_fusion
  237.0 1.0 collective-permute-done.45.refs_3_
  238.0 2.5 %adam.2 = (f32[192,2048]{1,0:T(8,128)}, f32[192,2048]{1,0:T(8,128)}, f32[192,2048]{1,0:T(8,128)}) custom-call(bf16[192,256]{1,0:T(8,128)(2,1)S(1)} %get-tuple-element.163.refs_0_, bf16[192,256]{1,0:T(8,128)(2,1)S(1)} %collective-permute-done.43.refs_1_, bf16[192,256]{1,0:T(8,128)(2,1)S(1)} %collective-permute-done.44.refs_2_, ...), custom_call_target="tpu_custom_call" | custom-call | tf_op jit(solution)/shard_map/adam/pallas_call | solution.py:687
  240.6 2.5 %adam.3 = (f32[192,2048]{1,0:T(8,128)}, f32[192,2048]{1,0:T(8,128)}, f32[192,2048]{1,0:T(8,128)}) custom-call(bf16[192,256]{1,0:T(8,128)(2,1)S(1)} %fourth_kernel.3.refs_0_, bf16[192,256]{1,0:T(8,128)(2,1)S(1)} %collective-permute-done.40.refs_1_, ...), custom_call_target="tpu_custom_call", output_to_operand_aliasing={{0}: (7, {}), {1}: (8, {}), {2}: (9, {})} | custom-call | tf_op jit(solution)/shard_map/adam/pallas_call | solution.py:687
  (149 shorter events, 9.0 us)
Async XLA Ops:
  1.7 10.4 %collective-permute-start = (bf16[192,256]{1,0:T(8,128)(2,1)S(1)}, bf16[192,256]{1,0:T(8,128)(2,1)S(1)}, u32[]{:S(2)}, u32[]{:S(2)}) collective-permute-start(bf16[192,256]{1,0:T(8,128)(2,1)S(1)} %get-tuple-element.176), channel_id=1, source_target_pairs={{0,8},{4,12},{8,16},{12,20},{16,24},{20,28},{24,0},{28,4},{1,9},{5... | collective-permute-start | bytes 294920 | tf_op jit(solution)/shard_map/ppermute | solution.py:710
  3.1 9.1 %collective-permute-start.1 = (bf16[192,256]{1,0:T(8,128)(2,1)S(1)}, bf16[192,256]{1,0:T(8,128)(2,1)S(1)}, u32[]{:S(2)}, u32[]{:S(2)}) collective-permute-start(bf16[192,256]{1,0:T(8,128)(2,1)S(1)} %get-tuple-element.176), channel_id=1, source_target_pairs={{0,16},{4,20},{8,24},{12,28},{16,0},{20,4},{24,8},{28,12},{1,17},{... | collective-permute-start | bytes 294920 | tf_op jit(solution)/shard_map/ppermute | solution.py:710
  3.1 9.0 %collective-permute-start.2 = (bf16[192,256]{1,0:T(8,128)(2,1)S(1)}, bf16[192,256]{1,0:T(8,128)(2,1)S(1)}, u32[]{:S(2)}, u32[]{:S(2)}) collective-permute-start(bf16[192,256]{1,0:T(8,128)(2,1)S(1)} %get-tuple-element.176), channel_id=1, source_target_pairs={{0,24},{4,28},{8,0},{12,4},{16,8},{20,12},{24,16},{28,20},{1,25},{... | collective-permute-start | bytes 294920 | tf_op jit(solution)/shard_map/ppermute | solution.py:710
  12.2 39.4 %copy-start.11 = (bf16[4,192,256]{2,1,0:T(8,128)(2,1)}, bf16[4,192,256]{2,1,0:T(8,128)(2,1)S(1)}, u32[]{:S(2)}) copy-start(bf16[4,192,256]{2,1,0:T(8,128)(2,1)S(1)} %pad_maximum_fusion.refs_0_) | copy-start | bytes 1179652
  12.2 9.4 %collective-permute-start.3 = (bf16[4,192,256]{2,1,0:T(8,128)(2,1)S(1)}, bf16[4,192,256]{2,1,0:T(8,128)(2,1)S(1)}, u32[]{:S(2)}, u32[]{:S(2)}) collective-permute-start(bf16[4,192,256]{2,1,0:T(8,128)(2,1)S(1)} %pad_maximum_fusion.refs_0_), channel_id=1, source_target_pairs={{0,4},{4,0},{8,12},{12,8},{16,20},{20,16},{24,28},{28,24},{1,5},{5... | collective-permute-start | bytes 1179656 | tf_op jit(solution)/shard_map/ppermute | solution.py:705
  13.5 8.9 %collective-permute-start.4 = (bf16[4,192,256]{2,1,0:T(8,128)(2,1)S(1)}, bf16[4,192,256]{2,1,0:T(8,128)(2,1)S(1)}, u32[]{:S(2)}, u32[]{:S(2)}) collective-permute-start(bf16[4,192,256]{2,1,0:T(8,128)(2,1)S(1)} %pad_maximum_fusion.refs_0_), channel_id=1, source_target_pairs={{0,2},{1,3},{2,0},{3,1},{4,6},{5,7},{6,4},{7,5},{8,10},{9,11},{10,... | collective-permute-start | bytes 1179656 | tf_op jit(solution)/shard_map/ppermute | solution.py:705
  14.7 7.8 %collective-permute-start.7 = (bf16[192,256]{1,0:T(8,128)(2,1)S(1)}, bf16[192,256]{1,0:T(8,128)(2,1)S(1)}, u32[]{:S(2)}, u32[]{:S(2)}) collective-permute-start(bf16[192,256]{1,0:T(8,128)(2,1)S(1)} %get-tuple-element.94), channel_id=1, source_target_pairs={{0,8},{4,12},{8,16},{12,20},{16,24},{20,28},{24,0},{28,4},{1,9},{5... | collective-permute-start | bytes 294920 | tf_op jit(solution)/shard_map/ppermute | solution.py:710
  15.3 8.5 %collective-permute-start.8 = (bf16[192,256]{1,0:T(8,128)(2,1)S(1)}, bf16[192,256]{1,0:T(8,128)(2,1)S(1)}, u32[]{:S(2)}, u32[]{:S(2)}) collective-permute-start(bf16[192,256]{1,0:T(8,128)(2,1)S(1)} %get-tuple-element.94), channel_id=1, source_target_pairs={{0,16},{4,20},{8,24},{12,28},{16,0},{20,4},{24,8},{28,12},{1,17},{... | collective-permute-start | bytes 294920 | tf_op jit(solution)/shard_map/ppermute | solution.py:710
  17.6 8.5 %collective-permute-start.9 = (bf16[192,256]{1,0:T(8,128)(2,1)S(1)}, bf16[192,256]{1,0:T(8,128)(2,1)S(1)}, u32[]{:S(2)}, u32[]{:S(2)}) collective-permute-start(bf16[192,256]{1,0:T(8,128)(2,1)S(1)} %get-tuple-element.94), channel_id=1, source_target_pairs={{0,24},{4,28},{8,0},{12,4},{16,8},{20,12},{24,16},{28,20},{1,25},{... | collective-permute-start | bytes 294920 | tf_op jit(solution)/shard_map/ppermute | solution.py:710
  21.7 29.9 %copy-start.15 = (bf16[4,192,256]{2,1,0:T(8,128)(2,1)}, bf16[4,192,256]{2,1,0:T(8,128)(2,1)S(1)}, u32[]{:S(2)}) copy-start(bf16[4,192,256]{2,1,0:T(8,128)(2,1)S(1)} %collective-permute-done.3.refs_1_) | copy-start | bytes 1179652
  22.5 29.2 %copy-start.16 = (bf16[4,192,256]{2,1,0:T(8,128)(2,1)}, bf16[4,192,256]{2,1,0:T(8,128)(2,1)S(1)}, u32[]{:S(2)}) copy-start(bf16[4,192,256]{2,1,0:T(8,128)(2,1)S(1)} %collective-permute-done.4.refs_2_) | copy-start | bytes 1179652
  26.2 25.5 %copy-start.12 = (bf16[4,192,256]{2,1,0:T(8,128)(2,1)}, bf16[4,192,256]{2,1,0:T(8,128)(2,1)S(1)}, u32[]{:S(2)}) copy-start(bf16[4,192,256]{2,1,0:T(8,128)(2,1)S(1)} %pad_maximum_fusion.1.refs_10_) | copy-start | bytes 1179652
  26.2 9.8 %collective-permute-start.10 = (bf16[4,192,256]{2,1,0:T(8,128)(2,1)S(1)}, bf16[4,192,256]{2,1,0:T(8,128)(2,1)S(1)}, u32[]{:S(2)}, u32[]{:S(2)}) collective-permute-start(bf16[4,192,256]{2,1,0:T(8,128)(2,1)S(1)} %pad_maximum_fusion.1.refs_10_), channel_id=1, source_target_pairs={{0,4},{4,0},{8,12},{12,8},{16,20},{20,16},{24,28},{28,24},{1,5},{5... | collective-permute-start | bytes 1179656 | tf_op jit(solution)/shard_map/ppermute | solution.py:705
  26.5 9.9 %collective-permute-start.11 = (bf16[4,192,256]{2,1,0:T(8,128)(2,1)S(1)}, bf16[4,192,256]{2,1,0:T(8,128)(2,1)S(1)}, u32[]{:S(2)}, u32[]{:S(2)}) collective-permute-start(bf16[4,192,256]{2,1,0:T(8,128)(2,1)S(1)} %pad_maximum_fusion.1.refs_10_), channel_id=1, source_target_pairs={{0,2},{1,3},{2,0},{3,1},{4,6},{5,7},{6,4},{7,5},{8,10},{9,11},{10,... | collective-permute-start | bytes 1179656 | tf_op jit(solution)/shard_map/ppermute | solution.py:705
  26.7 13.5 %collective-permute-start.5 = (bf16[4,192,128]{2,1,0:T(8,128)(2,1)S(1)}, bf16[4,192,128]{2,1,0:T(8,128)(2,1)S(1)}, u32[]{:S(2)}, u32[]{:S(2)}) collective-permute-start(bf16[4,192,128]{2,1,0:T(8,128)(2,1)S(1)} %slice.60), channel_id=1, source_target_pairs={{0,2},{1,3},{2,0},{3,1},{4,6},{5,7},{6,4},{7,5},{8,10},{9,11},{10,... | collective-permute-start | bytes 589832 | tf_op jit(solution)/shard_map/ppermute | solution.py:705
  28.0 12.3 %collective-permute-start.6 = (bf16[4,192,128]{2,1,0:T(8,128)(2,1)S(1)}, bf16[4,192,128]{2,1,0:T(8,128)(2,1)S(1)}, u32[]{:S(2)}, u32[]{:S(2)}) collective-permute-start(bf16[4,192,128]{2,1,0:T(8,128)(2,1)S(1)} %slice.61), channel_id=1, source_target_pairs={{0,4},{4,0},{8,12},{12,8},{16,20},{20,16},{24,28},{28,24},{1,5},{5... | collective-permute-start | bytes 589832 | tf_op jit(solution)/shard_map/ppermute | solution.py:705
  36.0 15.6 %copy-start.17 = (bf16[4,192,256]{2,1,0:T(8,128)(2,1)}, bf16[4,192,256]{2,1,0:T(8,128)(2,1)S(1)}, u32[]{:S(2)}) copy-start(bf16[4,192,256]{2,1,0:T(8,128)(2,1)S(1)} %collective-permute-done.10.refs_11_) | copy-start | bytes 1179652
  36.1 8.4 %collective-permute-start.17 = (bf16[4,192,128]{2,1,0:T(8,128)(2,1)S(1)}, bf16[4,192,128]{2,1,0:T(8,128)(2,1)S(1)}, u32[]{:S(2)}, u32[]{:S(2)}) collective-permute-start(bf16[4,192,128]{2,1,0:T(8,128)(2,1)S(1)} %slice.62), channel_id=1, source_target_pairs={{0,2},{1,3},{2,0},{3,1},{4,6},{5,7},{6,4},{7,5},{8,10},{9,11},{10,... | collective-permute-start | bytes 589832 | tf_op jit(solution)/shard_map/ppermute | solution.py:705
  36.3 15.3 %copy-start.18 = (bf16[4,192,256]{2,1,0:T(8,128)(2,1)}, bf16[4,192,256]{2,1,0:T(8,128)(2,1)S(1)}, u32[]{:S(2)}) copy-start(bf16[4,192,256]{2,1,0:T(8,128)(2,1)S(1)} %collective-permute-done.11.refs_12_) | copy-start | bytes 1179652
  36.4 8.1 %collective-permute-start.18 = (bf16[4,192,128]{2,1,0:T(8,128)(2,1)S(1)}, bf16[4,192,128]{2,1,0:T(8,128)(2,1)S(1)}, u32[]{:S(2)}, u32[]{:S(2)}) collective-permute-start(bf16[4,192,128]{2,1,0:T(8,128)(2,1)S(1)} %slice.63), channel_id=1, source_target_pairs={{0,4},{4,0},{8,12},{12,8},{16,20},{20,16},{24,28},{28,24},{1,5},{5... | collective-permute-start | bytes 589832 | tf_op jit(solution)/shard_map/ppermute | solution.py:705
  40.2 10.6 %copy-start.30 = (bf16[4,192,128]{2,1,0:T(8,128)(2,1)}, bf16[4,192,128]{2,1,0:T(8,128)(2,1)S(1)}, u32[]{:S(2)}) copy-start(bf16[4,192,128]{2,1,0:T(8,128)(2,1)S(1)} %collective-permute-done.5.refs_3_) | copy-start | bytes 589828
  40.2 10.6 %copy-start.31 = (bf16[4,192,128]{2,1,0:T(8,128)(2,1)}, bf16[4,192,128]{2,1,0:T(8,128)(2,1)S(1)}, u32[]{:S(2)}) copy-start(bf16[4,192,128]{2,1,0:T(8,128)(2,1)S(1)} %collective-permute-done.6.refs_4_) | copy-start | bytes 589828
  40.2 8.0 %collective-permute-start.12 = (bf16[4,192,256]{2,1,0:T(8,128)(2,1)S(1)}, bf16[4,192,256]{2,1,0:T(8,128)(2,1)S(1)}, u32[]{:S(2)}, u32[]{:S(2)}) collective-permute-start(bf16[4,192,256]{2,1,0:T(8,128)(2,1)S(1)} %pad_maximum_fusion.refs_0_), channel_id=1, source_target_pairs={{0,1},{1,0},{2,3},{3,2},{4,5},{5,4},{6,7},{7,6},{8,9},{9,8},{10,11... | collective-permute-start | bytes 1179656 | tf_op jit(solution)/shard_map/ppermute | solution.py:705
  44.0 2.6 %collective-permute-start.15 = (bf16[4,192,128]{2,1,0:T(8,128)(2,1)S(1)}, bf16[4,192,128]{2,1,0:T(8,128)(2,1)S(1)}, u32[]{:S(2)}, u32[]{:S(2)}) collective-permute-start(bf16[4,192,128]{2,1,0:T(8,128)(2,1)S(1)} %collective-permute-done.5.refs_3_), channel_id=1, source_target_pairs={{0,1},{1,0},{2,3},{3,2},{4,5},{5,4},{6,7},{7,6},{8,9},{9,8},{10,11... | collective-permute-start | bytes 589832 | tf_op jit(solution)/shard_map/ppermute | solution.py:705
  44.0 3.0 %collective-permute-start.16 = (bf16[4,192,128]{2,1,0:T(8,128)(2,1)S(1)}, bf16[4,192,128]{2,1,0:T(8,128)(2,1)S(1)}, u32[]{:S(2)}, u32[]{:S(2)}) collective-permute-start(bf16[4,192,128]{2,1,0:T(8,128)(2,1)S(1)} %collective-permute-done.6.refs_4_), channel_id=1, source_target_pairs={{0,1},{1,0},{2,3},{3,2},{4,5},{5,4},{6,7},{7,6},{8,9},{9,8},{10,11... | collective-permute-start | bytes 589832 | tf_op jit(solution)/shard_map/ppermute | solution.py:705
  44.5 6.3 %copy-start.32 = (bf16[4,192,128]{2,1,0:T(8,128)(2,1)}, bf16[4,192,128]{2,1,0:T(8,128)(2,1)S(1)}, u32[]{:S(2)}) copy-start(bf16[4,192,128]{2,1,0:T(8,128)(2,1)S(1)} %collective-permute-done.17.refs_13_) | copy-start | bytes 589828
  44.5 6.3 %copy-start.33 = (bf16[4,192,128]{2,1,0:T(8,128)(2,1)}, bf16[4,192,128]{2,1,0:T(8,128)(2,1)S(1)}, u32[]{:S(2)}) copy-start(bf16[4,192,128]{2,1,0:T(8,128)(2,1)S(1)} %collective-permute-done.18.refs_14_) | copy-start | bytes 589828
  44.5 3.1 %collective-permute-start.22 = (bf16[4,192,128]{2,1,0:T(8,128)(2,1)S(1)}, bf16[4,192,128]{2,1,0:T(8,128)(2,1)S(1)}, u32[]{:S(2)}, u32[]{:S(2)}) collective-permute-start(bf16[4,192,128]{2,1,0:T(8,128)(2,1)S(1)} %collective-permute-done.17.refs_13_), channel_id=1, source_target_pairs={{0,1},{1,0},{2,3},{3,2},{4,5},{5,4},{6,7},{7,6},{8,9},{9,8},{10,11... | collective-permute-start | bytes 589832 | tf_op jit(solution)/shard_map/ppermute | solution.py:705
  46.5 1.5 collective-permute-start.23
  46.6 2.0 collective-permute-start.13
  47.0 2.0 collective-permute-start.14
  47.6 2.1 collective-permute-start.19
  48.0 2.8 %collective-permute-start.20 = (bf16[4,192,256]{2,1,0:T(8,128)(2,1)S(1)}, bf16[4,192,256]{2,1,0:T(8,128)(2,1)S(1)}, u32[]{:S(2)}, u32[]{:S(2)}) collective-permute-start(bf16[4,192,256]{2,1,0:T(8,128)(2,1)S(1)} %collective-permute-done.10.refs_11_), channel_id=1, source_target_pairs={{0,1},{1,0},{2,3},{3,2},{4,5},{5,4},{6,7},{7,6},{8,9},{9,8},{10,11... | collective-permute-start | bytes 1179656 | tf_op jit(solution)/shard_map/ppermute | solution.py:705
  48.2 3.3 %collective-permute-start.21 = (bf16[4,192,256]{2,1,0:T(8,128)(2,1)S(1)}, bf16[4,192,256]{2,1,0:T(8,128)(2,1)}, u32[]{:S(2)}, u32[]{:S(2)}) collective-permute-start(bf16[4,192,256]{2,1,0:T(8,128)(2,1)S(1)} %collective-permute-done.11.refs_12_), channel_id=1, source_target_pairs={{0,1},{1,0},{2,3},{3,2},{4,5},{5,4},{6,7},{7,6},{8,9},{9,8},{10,11... | collective-permute-start | bytes 1179656 | tf_op jit(solution)/shard_map/ppermute | solution.py:705
  175.9 3.5 %collective-permute-start.27 = (bf16[1536,512]{1,0:T(8,128)(2,1)S(1)}, bf16[1536,512]{1,0:T(8,128)(2,1)S(1)}, u32[]{:S(2)}, u32[]{:S(2)}) collective-permute-start(bf16[1536,512]{1,0:T(8,128)(2,1)S(1)} %convolution_convert_fusion), channel_id=1, source_target_pairs={{0,1},{1,0},{2,3},{3,2},{4,5},{5,4},{6,7},{7,6},{8,9},{9,8},{10,11... | collective-permute-start | bytes 4718600 | tf_op jit(solution)/shard_map/ppermute | solution.py:705
  178.1 4.9 %collective-permute-start.24 = (bf16[1536,512]{1,0:T(8,128)(2,1)S(1)}, bf16[1536,512]{1,0:T(8,128)(2,1)S(1)}, u32[]{:S(2)}, u32[]{:S(2)}) collective-permute-start(bf16[1536,512]{1,0:T(8,128)(2,1)S(1)} %convolution_convert_fusion.1), channel_id=1, source_target_pairs={{0,1},{1,0},{2,3},{3,2},{4,5},{5,4},{6,7},{7,6},{8,9},{9,8},{10,11... | collective-permute-start | bytes 4718600 | tf_op jit(solution)/shard_map/ppermute | solution.py:705
  181.4 11.0 %collective-permute-start.28 = (bf16[1632,128]{1,0:T(8,128)(2,1)S(1)}, bf16[1632,128]{1,0:T(8,128)(2,1)S(1)}, u32[]{:S(2)}, u32[]{:S(2)}) collective-permute-start(bf16[1632,128]{1,0:T(8,128)(2,1)S(1)} %get-tuple-element.118), channel_id=1, source_target_pairs={{0,2},{1,3},{2,0},{3,1},{4,6},{5,7},{6,4},{7,5},{8,10},{9,11},{10,... | collective-permute-start | bytes 1253384 | tf_op jit(solution)/shard_map/ppermute | solution.py:705
  181.8 10.2 %collective-permute-start.29 = (bf16[4,192,256]{2,1,0:T(8,128)(2,1)S(1)}, bf16[4,192,256]{2,1,0:T(8,128)(2,1)S(1)}, u32[]{:S(2)}, u32[]{:S(2)}) collective-permute-start(bf16[4,192,256]{2,1,0:T(8,128)(2,1)S(1)} %get-tuple-element.119), channel_id=1, source_target_pairs={{0,4},{4,0},{8,12},{12,8},{16,20},{20,16},{24,28},{28,24},{1,5},{5... | collective-permute-start | bytes 1179656 | tf_op jit(solution)/shard_map/ppermute | solution.py:705
  185.0 15.8 %collective-permute-start.25 = (bf16[1536,128]{1,0:T(8,128)(2,1)S(1)}, bf16[1536,128]{1,0:T(8,128)(2,1)S(1)}, u32[]{:S(2)}, u32[]{:S(2)}) collective-permute-start(bf16[1536,128]{1,0:T(8,128)(2,1)S(1)} %get-tuple-element.115), channel_id=1, source_target_pairs={{0,2},{1,3},{2,0},{3,1},{4,6},{5,7},{6,4},{7,5},{8,10},{9,11},{10,... | collective-permute-start | bytes 1179656 | tf_op jit(solution)/shard_map/ppermute | solution.py:705
  186.2 14.6 %collective-permute-start.26 = (bf16[4,192,256]{2,1,0:T(8,128)(2,1)S(1)}, bf16[4,192,256]{2,1,0:T(8,128)(2,1)S(1)}, u32[]{:S(2)}, u32[]{:S(2)}) collective-permute-start(bf16[4,192,256]{2,1,0:T(8,128)(2,1)S(1)} %get-tuple-element.116), channel_id=1, source_target_pairs={{0,4},{4,0},{8,12},{12,8},{16,20},{20,16},{24,28},{28,24},{1,5},{5... | collective-permute-start | bytes 1179656 | tf_op jit(solution)/shard_map/ppermute | solution.py:705
  192.7 12.5 %collective-permute-start.32 = (bf16[864,128]{1,0:T(8,128)(2,1)S(1)}, bf16[864,128]{1,0:T(8,128)(2,1)S(1)}, u32[]{:S(2)}, u32[]{:S(2)}) collective-permute-start(bf16[864,128]{1,0:T(8,128)(2,1)S(1)} %get-tuple-element.120), channel_id=1, source_target_pairs={{0,4},{4,0},{8,12},{12,8},{16,20},{20,16},{24,28},{28,24},{1,5},{5... | collective-permute-start | bytes 663560 | tf_op jit(solution)/shard_map/ppermute | solution.py:705
  194.0 11.1 %collective-permute-start.33 = (bf16[4,192,128]{2,1,0:T(8,128)(2,1)S(1)}, bf16[4,192,128]{2,1,0:T(8,128)(2,1)S(1)}, u32[]{:S(2)}, u32[]{:S(2)}) collective-permute-start(bf16[4,192,128]{2,1,0:T(8,128)(2,1)S(1)} %get-tuple-element.121), channel_id=1, source_target_pairs={{0,2},{1,3},{2,0},{3,1},{4,6},{5,7},{6,4},{7,5},{8,10},{9,11},{10,... | collective-permute-start | bytes 589832 | tf_op jit(solution)/shard_map/ppermute | solution.py:705
  201.1 12.1 %copy-start.4 = (bf16[512,2048]{1,0:T(8,128)(2,1)S(1)}, bf16[512,2048]{1,0:T(8,128)(2,1)}, u32[]{:S(2)}) copy-start(bf16[512,2048]{1,0:T(8,128)(2,1)} %get-tuple-element.147) | copy-start | bytes 6291460
  201.1 8.2 %collective-permute-start.30 = (bf16[768,128]{1,0:T(8,128)(2,1)S(1)}, bf16[768,128]{1,0:T(8,128)(2,1)S(1)}, u32[]{:S(2)}, u32[]{:S(2)}) collective-permute-start(bf16[768,128]{1,0:T(8,128)(2,1)S(1)} %get-tuple-element.126), channel_id=1, source_target_pairs={{0,4},{4,0},{8,12},{12,8},{16,20},{20,16},{24,28},{28,24},{1,5},{5... | collective-permute-start | bytes 589832 | tf_op jit(solution)/shard_map/ppermute | solution.py:705
  202.4 7.0 %collective-permute-start.31 = (bf16[4,192,128]{2,1,0:T(8,128)(2,1)S(1)}, bf16[4,192,128]{2,1,0:T(8,128)(2,1)S(1)}, u32[]{:S(2)}, u32[]{:S(2)}) collective-permute-start(bf16[4,192,128]{2,1,0:T(8,128)(2,1)S(1)} %get-tuple-element.127), channel_id=1, source_target_pairs={{0,2},{1,3},{2,0},{3,1},{4,6},{5,7},{6,4},{7,5},{8,10},{9,11},{10,... | collective-permute-start | bytes 589832 | tf_op jit(solution)/shard_map/ppermute | solution.py:705
  205.3 15.9 %collective-permute-start.37 = (bf16[240,256]{1,0:T(8,128)(2,1)S(1)}, bf16[240,256]{1,0:T(8,128)(2,1)S(1)}, u32[]{:S(2)}, u32[]{:S(2)}) collective-permute-start(bf16[240,256]{1,0:T(8,128)(2,1)S(1)} %get-tuple-element.133), channel_id=1, source_target_pairs={{0,8},{4,12},{8,16},{12,20},{16,24},{20,28},{24,0},{28,4},{1,9},{5... | collective-permute-start | bytes 368648 | tf_op jit(solution)/shard_map/ppermute | solution.py:710
  207.2 13.9 %collective-permute-start.38 = (bf16[240,256]{1,0:T(8,128)(2,1)S(1)}, bf16[240,256]{1,0:T(8,128)(2,1)S(1)}, u32[]{:S(2)}, u32[]{:S(2)}) collective-permute-start(bf16[240,256]{1,0:T(8,128)(2,1)S(1)} %get-tuple-element.134), channel_id=1, source_target_pairs={{0,16},{4,20},{8,24},{12,28},{16,0},{20,4},{24,8},{28,12},{1,17},{... | collective-permute-start | bytes 368648 | tf_op jit(solution)/shard_map/ppermute | solution.py:710
  208.7 13.4 %collective-permute-start.39 = (bf16[240,256]{1,0:T(8,128)(2,1)S(1)}, bf16[240,256]{1,0:T(8,128)(2,1)S(1)}, u32[]{:S(2)}, u32[]{:S(2)}) collective-permute-start(bf16[240,256]{1,0:T(8,128)(2,1)S(1)} %get-tuple-element.135), channel_id=1, source_target_pairs={{0,24},{4,28},{8,0},{12,4},{16,8},{20,12},{24,16},{28,20},{1,25},{... | collective-permute-start | bytes 368648 | tf_op jit(solution)/shard_map/ppermute | solution.py:710
  209.5 11.2 %collective-permute-start.34 = (bf16[192,256]{1,0:T(8,128)(2,1)S(1)}, bf16[192,256]{1,0:T(8,128)(2,1)S(1)}, u32[]{:S(2)}, u32[]{:S(2)}) collective-permute-start(bf16[192,256]{1,0:T(8,128)(2,1)S(1)} %get-tuple-element.140), channel_id=1, source_target_pairs={{0,8},{4,12},{8,16},{12,20},{16,24},{20,28},{24,0},{28,4},{1,9},{5... | collective-permute-start | bytes 294920 | tf_op jit(solution)/shard_map/ppermute | solution.py:710
  211.7 12.6 %collective-permute-start.35 = (bf16[192,256]{1,0:T(8,128)(2,1)S(1)}, bf16[192,256]{1,0:T(8,128)(2,1)S(1)}, u32[]{:S(2)}, u32[]{:S(2)}) collective-permute-start(bf16[192,256]{1,0:T(8,128)(2,1)S(1)} %get-tuple-element.141), channel_id=1, source_target_pairs={{0,16},{4,20},{8,24},{12,28},{16,0},{20,4},{24,8},{28,12},{1,17},{... | collective-permute-start | bytes 294920 | tf_op jit(solution)/shard_map/ppermute | solution.py:710
  216.8 21.3 %copy-start.2 = (f32[192,2048]{1,0:T(8,128)S(1)}, f32[192,2048]{1,0:T(8,128)}, u32[]{:S(2)}) copy-start(f32[192,2048]{1,0:T(8,128)} %refs_6_.3) | copy-start | bytes 4718596
  219.3 17.0 %copy-start.14 = (f32[5632]{0:T(1024)S(1)}, f32[5632]{0:T(1024)}, u32[]{:S(2)}) copy-start(f32[5632]{0:T(1024)} %param.23) | copy-start | bytes 67588
  219.3 17.0 %copy-start.21 = (f32[5632]{0:T(1024)S(1)}, f32[5632]{0:T(1024)}, u32[]{:S(2)}) copy-start(f32[5632]{0:T(1024)} %param.24) | copy-start | bytes 67588
  219.3 17.0 %copy-start.22 = (f32[5632]{0:T(1024)S(1)}, f32[5632]{0:T(1024)}, u32[]{:S(2)}) copy-start(f32[5632]{0:T(1024)} %param.25) | copy-start | bytes 67588
  219.3 18.7 %copy-start = (f32[192,2048]{1,0:T(8,128)S(1)}, f32[192,2048]{1,0:T(8,128)}, u32[]{:S(2)}) copy-start(f32[192,2048]{1,0:T(8,128)} %refs_4_.3) | copy-start | bytes 4718596
  219.3 18.7 %copy-start.1 = (f32[192,2048]{1,0:T(8,128)S(1)}, f32[192,2048]{1,0:T(8,128)}, u32[]{:S(2)}) copy-start(f32[192,2048]{1,0:T(8,128)} %refs_5_.3) | copy-start | bytes 4718596
  220.7 5.5 %collective-permute-start.36 = (bf16[192,256]{1,0:T(8,128)(2,1)S(1)}, bf16[192,256]{1,0:T(8,128)(2,1)S(1)}, u32[]{:S(2)}, u32[]{:S(2)}) collective-permute-start(bf16[192,256]{1,0:T(8,128)(2,1)S(1)} %get-tuple-element.142), channel_id=1, source_target_pairs={{0,24},{4,28},{8,0},{12,4},{16,8},{20,12},{24,16},{28,20},{1,25},{... | collective-permute-start | bytes 294920 | tf_op jit(solution)/shard_map/ppermute | solution.py:710
  222.2 4.5 %collective-permute-start.43 = (bf16[192,256]{1,0:T(8,128)(2,1)S(1)}, bf16[192,256]{1,0:T(8,128)(2,1)S(1)}, u32[]{:S(2)}, u32[]{:S(2)}) collective-permute-start(bf16[192,256]{1,0:T(8,128)(2,1)S(1)} %get-tuple-element.163.refs_0_), channel_id=1, source_target_pairs={{0,2},{1,3},{2,0},{3,1},{4,6},{5,7},{6,4},{7,5},{8,10},{9,11},{10,... | collective-permute-start | bytes 294920 | tf_op jit(solution)/shard_map/ppermute | solution.py:705
  226.2 7.8 %collective-permute-start.40 = (bf16[192,256]{1,0:T(8,128)(2,1)S(1)}, bf16[192,256]{1,0:T(8,128)(2,1)S(1)}, u32[]{:S(2)}, u32[]{:S(2)}) collective-permute-start(bf16[192,256]{1,0:T(8,128)(2,1)S(1)} %fourth_kernel.3.refs_0_), channel_id=1, source_target_pairs={{0,2},{1,3},{2,0},{3,1},{4,6},{5,7},{6,4},{7,5},{8,10},{9,11},{10,... | collective-permute-start | bytes 294920 | tf_op jit(solution)/shard_map/ppermute | solution.py:705
  226.7 9.6 %collective-permute-start.46 = (bf16[48,256]{1,0:T(8,128)(2,1)S(1)}, bf16[48,256]{1,0:T(8,128)(2,1)S(1)}, u32[]{:S(2)}, u32[]{:S(2)}) collective-permute-start(bf16[48,256]{1,0:T(8,128)(2,1)S(1)} %get-tuple-element.171), channel_id=1, source_target_pairs={{0,1},{1,0},{2,3},{3,2},{4,5},{5,4},{6,7},{7,6},{8,9},{9,8},{10,11... | collective-permute-start | bytes 73736 | tf_op jit(solution)/shard_map/ppermute | solution.py:705
  232.1 5.9 %collective-permute-start.45 = (bf16[192,256]{1,0:T(8,128)(2,1)S(1)}, bf16[192,256]{1,0:T(8,128)(2,1)S(1)}, u32[]{:S(2)}, u32[]{:S(2)}) collective-permute-start(bf16[192,256]{1,0:T(8,128)(2,1)S(1)} %get-tuple-element.163.refs_0_), channel_id=1, source_target_pairs={{0,3},{1,2},{2,1},{3,0},{4,7},{5,6},{6,5},{7,4},{8,11},{9,10},{10,... | collective-permute-start | bytes 294920 | tf_op jit(solution)/shard_map/ppermute | solution.py:705
  232.8 7.8 %collective-permute-start.42 = (bf16[192,256]{1,0:T(8,128)(2,1)S(1)}, bf16[192,256]{1,0:T(8,128)(2,1)S(1)}, u32[]{:S(2)}, u32[]{:S(2)}) collective-permute-start(bf16[192,256]{1,0:T(8,128)(2,1)S(1)} %fourth_kernel.3.refs_0_), channel_id=1, source_target_pairs={{0,3},{1,2},{2,1},{3,0},{4,7},{5,6},{6,5},{7,4},{8,11},{9,10},{10,... | collective-permute-start | bytes 294920 | tf_op jit(solution)/shard_map/ppermute | solution.py:705
  233.9 4.2 %collective-permute-start.44 = (bf16[192,256]{1,0:T(8,128)(2,1)S(1)}, bf16[192,256]{1,0:T(8,128)(2,1)S(1)}, u32[]{:S(2)}, u32[]{:S(2)}) collective-permute-start(bf16[192,256]{1,0:T(8,128)(2,1)S(1)} %get-tuple-element.163.refs_0_), channel_id=1, source_target_pairs={{0,1},{1,0},{2,3},{3,2},{4,5},{5,4},{6,7},{7,6},{8,9},{9,8},{10,11... | collective-permute-start | bytes 294920 | tf_op jit(solution)/shard_map/ppermute | solution.py:705
  233.9 6.6 %collective-permute-start.41 = (bf16[192,256]{1,0:T(8,128)(2,1)S(1)}, bf16[192,256]{1,0:T(8,128)(2,1)S(1)}, u32[]{:S(2)}, u32[]{:S(2)}) collective-permute-start(bf16[192,256]{1,0:T(8,128)(2,1)S(1)} %fourth_kernel.3.refs_0_), channel_id=1, source_target_pairs={{0,1},{1,0},{2,3},{3,2},{4,5},{5,4},{6,7},{7,6},{8,9},{9,8},{10,11... | collective-permute-start | bytes 294920 | tf_op jit(solution)/shard_map/ppermute | solution.py:705
  (23 other events, 52.8 us)
where the time goes:
time: 244 us; the launch traced here: 243 us
  Pallas kernels  126 us (52%)
  starting transfers between devices  47.7 us (20%)
  waiting for transfers between devices  40.4 us (17%)
  matrix products  12.7 us (5%)
  local copies, waits for them, and re-layouts  8.8 us (4%)
  other arithmetic  6.17 us (3%)
    pallas_call x1, Pallas kernels, sweep(): pl.pallas_call(functools.partial(sweep_kernel, rows, blocks, described),...  120 us
    ppermute x35, starting transfers between devices, swap(): lax.ppermute(array, axis, [(index, index ^ bit) for index in range(count)])  32.4 us
    ppermute x35, waiting for transfers between devices, swap(): lax.ppermute(array, axis, [(index, index ^ bit) for index in range(count)])  32.2 us
    ppermute x12, starting transfers between devices, along_z(): lax.ppermute(array, 'dp', [(index, (index + 2 * step) % count) for index...  15.2 us
    dot_general x4, matrix products, product(): lax.dot_general(left, right, (((0,), (0,)), ((), ())), preferred_element_...  9.7 us
    ppermute x12, waiting for transfers between devices, along_z(): lax.ppermute(array, 'dp', [(index, (index + 2 * step) % count) for index...  8.24 us
    pallas_call x2, Pallas kernels, adam_columns(): pl.pallas_call(functools.partial(adam_kernel, chunk), in_specs=[in_vmem]...  5.01 us
  transfers between devices with their start and end apart: 47, of which 21 were waited for; matrix products, arithmetic and copies ran while one was open for 9% of the time, Pallas kernels for 1%

commit v1 on v0

--- a/solution.py
+++ b/solution.py
@@ -1016,14 +1016,11 @@
     sums, small_pair, (hidden, input_grad) = reduce_rows(totals, grad_small, late, late_inputs)
     weights = ()
     for chunk, grad in enumerate(sums):
-        far = swap(grad, PLANE)
-        grads = [grad, far, swap(after(grad, far), CORE), swap(grad, CORE | PLANE)]
-        if chunk == 0:
-            near_pair = swap(after(small_pair, far), CORE)
+        grads = [grad] + [swap(grad, bits) for bits in (PLANE, CORE, CORE | PLANE)]
         weights = adam_columns(chunk, grads, gate_weight, gate_m, gate_v, weights)
     weight_new, weight_m, weight_v = weights
     small_total = 0.0
-    for pair in (small_pair, near_pair):
+    for pair in (small_pair, swap(small_pair, CORE)):
         small_total = small_total + joined(pair[:, :LANES], pair[:, LANES:])
     small_total = small_total.reshape(-1)[: small_params.shape[0]]
 

time: 244 us -> 242 us (level)
  waiting for transfers between devices: 40.4 us -> 37.1 us
    ppermute x12, waiting for transfers between devices: 8.24 us -> 4.6 us  [along_z(): lax.ppermute(array, 'dp', [(index, (index + 2 * step) % count) for index...]
  transfers between devices with their start and end apart: 47 -> 47, of which waited for: 21 -> 20; matrix products, arithmetic and copies ran while one was open for 9% -> 9% of each run, Pallas kernels for 1% -> 1%
where the time goes in v1:
time: 242 us; the launch traced here: 240 us
  Pallas kernels  126 us (52%)
  starting transfers between devices  47.8 us (20%)
  waiting for transfers between devices  37.1 us (15%)
  matrix products  12.7 us (5%)
  local copies, waits for them, and re-layouts  8.8 us (4%)
  other arithmetic  6.17 us (3%)
    pallas_call x1, Pallas kernels, sweep(): pl.pallas_call(functools.partial(sweep_kernel, rows, blocks, described),...  120 us
    ppermute x35, starting transfers between devices, swap(): lax.ppermute(array, axis, [(index, index ^ bit) for index in range(count)])  32.6 us
    ppermute x35, waiting for transfers between devices, swap(): lax.ppermute(array, axis, [(index, index ^ bit) for index in range(count)])  32.5 us
    ppermute x12, starting transfers between devices, along_z(): lax.ppermute(array, 'dp', [(index, (index + 2 * step) % count) for index...  15.2 us
    dot_general x4, matrix products, product(): lax.dot_general(left, right, (((0,), (0,)), ((), ())), preferred_element_...  9.7 us
    pallas_call x2, Pallas kernels, adam_columns(): pl.pallas_call(functools.partial(adam_kernel, chunk), in_specs=[in_vmem]...  4.99 us
  transfers between devices with their start and end apart: 47, of which 20 were waited for; matrix products, arithmetic and copies ran while one was open for 9% of the time, Pallas kernels for 1%

profile of v1, /device:TPU:17, one launch (start us, length us, event | category | flops | bytes accessed | tf_op | source)
XLA Modules:
  0.0 240.1 jit_solution(12624106406140700295)
XLA Ops:
  0.7 1.1 dynamic-slice_convert_fusion
  1.7 1.3 collective-permute-start
  3.1 1.2 collective-permute-start.2
  4.3 1.3 fusion.16
  5.8 4.1 %copy_bitcast_fusion.1 = (bf16[1024,512]{1,0:T(8,128)(2,1)}, bf16[1024,512]{1,0:T(8,128)(2,1)}) fusion(bf16[128,8,512]{2,0,1:T(8,128)(2,1)} %bitcast.56, bf16[128,8,512]{2,0,1:T(8,128)(2,1)} %bitcast.57), kind=kLoop, calls=%fused_computation.8 | loop fusion | bytes 4194304 | tf_op jit(solution)/shard_map/reshape | solution.py:974
  9.9 1.6 bitcast_multiply_fusion.refs_20_
  11.5 0.6 broadcast_in_dim.5.refs_27_
  12.2 1.3 collective-permute-start.3
  13.5 1.2 collective-permute-start.4
  14.7 0.6 collective-permute-start.7
  15.3 2.3 collective-permute-start.8
  17.6 1.6 collective-permute-start.9
  19.3 2.4 collective-permute-done.3.refs_1_
  21.7 0.7 collective-permute-done.4.refs_2_
  22.5 1.4 collective-permute-done.8
  23.9 2.2 collective-permute-done.9
  26.7 1.2 collective-permute-start.5
  28.0 1.2 collective-permute-start.6
  29.2 6.8 %collective-permute-done.10.refs_11_ = bf16[4,192,256]{2,1,0:T(8,128)(2,1)S(1)} collective-permute-done((bf16[4,192,256]{2,1,0:T(8,128)(2,1)S(1)}, bf16[4,192,256]{2,1,0:T(8,128)(2,1)S(1)}, u32[]{:S(2)}, u32[]{:S(2)}) %collective-permute-start.10) | collective-permute-done | bytes 393248 | tf_op jit(solution)/shard_map/ppermute | solution.py:705
  36.4 0.9 collective-permute-start.18
  37.3 2.9 %collective-permute-done.5.refs_3_ = bf16[4,192,128]{2,1,0:T(8,128)(2,1)S(1)} collective-permute-done((bf16[4,192,128]{2,1,0:T(8,128)(2,1)S(1)}, bf16[4,192,128]{2,1,0:T(8,128)(2,1)S(1)}, u32[]{:S(2)}, u32[]{:S(2)}) %collective-permute-start.5) | collective-permute-done | bytes 196640 | tf_op jit(solution)/shard_map/ppermute | solution.py:705
  40.2 3.7 %collective-permute-start.12 = (bf16[4,192,256]{2,1,0:T(8,128)(2,1)S(1)}, bf16[4,192,256]{2,1,0:T(8,128)(2,1)S(1)}, u32[]{:S(2)}, u32[]{:S(2)}) collective-permute-start(bf16[4,192,256]{2,1,0:T(8,128)(2,1)S(1)} %pad_maximum_fusion.refs_0_), channel_id=1, source_target_pairs={{0,1},{1,0},{2,3},{3,2},{4,5},{5,4},{6,7},{7,6},{8,9},{9,8},{10,11... | collective-permute-start | bytes 1179656 | tf_op jit(solution)/shard_map/ppermute | solution.py:705
  44.5 2.0 collective-permute-start.22
  48.6 0.5 collective-permute-done.14.refs_7_
  49.1 0.6 collective-permute-done.19.refs_15_
  49.7 1.1 collective-permute-done.20.refs_16_
  50.8 0.8 copy-done.29
  51.7 120.0 %sweep.1 = (bf16[1024,1536]{1,0:T(8,128)(2,1)}, bf16[1024,512]{1,0:T(8,128)(2,1)}, f32[8,512]{1,0:T(8,128)}, f32[8,128]{1,0:T(8,128)}, bf16[512,2048]{1,0:T(8,12...) custom-call(bf16[4,192,256]{2,1,0:T(8,128)(2,1)} %copy-done.11, ...), custom_call_target="tpu_custom_call" | custom-call | flops 130000003072 | bytes 100000000 | tf_op jit(solution)/shard_map/sweep/pallas_call | solution.py:624
  171.7 4.2 %convolution_convert_fusion = bf16[1536,512]{1,0:T(8,128)(2,1)S(1)} fusion(bf16[1024,1536]{1,0:T(8,128)(2,1)} %get-tuple-element.111, bf16[1024,512]{1,0:T(8,128)(2,1)} %get-tuple-element.146), kind=kOutput, calls=%fused_computation.2 | convolution fusion | flops 1611399168 | bytes 5767168 | tf_op jit(solution)/shard_map/dot_general | solution.py:996
  176.3 1.8 convolution_convert_fusion.1
  178.4 1.0 collective-permute-done.27
  179.4 1.9 convolution_add_fusion
  181.8 1.2 collective-permute-start.29
  183.0 1.9 convolution_add_fusion.1
  185.0 1.2 collective-permute-start.25
  186.5 5.5 %collective-permute-done.29.from_x_ref = bf16[4,192,256]{2,1,0:T(8,128)(2,1)S(1)} collective-permute-done((bf16[4,192,256]{2,1,0:T(8,128)(2,1)S(1)}, bf16[4,192,256]{2,1,0:T(8,128)(2,1)S(1)}, u32[]{:S(2)}, u32[]{:S(2)}) %collective-permute-start.29) | collective-permute-done | bytes 393248 | tf_op jit(solution)/shard_map/ppermute | solution.py:705
  192.7 1.3 collective-permute-start.32
  194.0 0.6 collective-permute-start.33
  194.6 6.3 %collective-permute-done.25.from_y_ref = bf16[1536,128]{1,0:T(8,128)(2,1)S(1)} collective-permute-done((bf16[1536,128]{1,0:T(8,128)(2,1)S(1)}, bf16[1536,128]{1,0:T(8,128)(2,1)S(1)}, u32[]{:S(2)}, u32[]{:S(2)}) %collective-permute-start.25) | collective-permute-done | bytes 393248 | tf_op jit(solution)/shard_map/ppermute | solution.py:705
  201.1 1.3 collective-permute-start.30
  202.4 0.6 collective-permute-start.31
  203.0 2.1 collective-permute-done.33.from_y_ref
  205.3 1.9 collective-permute-start.37
  207.2 1.5 collective-permute-start.38
  209.5 2.2 collective-permute-start.34
  211.7 1.5 collective-permute-start.35
  213.2 0.7 fusion.6
  213.9 0.7 fusion.8
  215.2 0.7 fusion.4
  216.0 0.8 multiply_bitcast_fusion
  216.8 2.6 %bitcast_add_fusion = f32[8,128,512]{2,1,0:T(8,128)} fusion(f32[128,8,512]{2,1,0:T(8,128)S(1)} %multiply_bitcast_fusion, f32[512]{0:T(512)S(1)} %slice-done, f32[8,128]{1,0:T(8,128)S(1)} %convert_multiply_fusion), kind=kLoop, calls=%fused_computation.4 | loop fusion | flops 1048576 | bytes 4200448 | tf_op jit(solution)/shard_map/add | solution.py:1012
  219.4 1.3 copy.42
  220.7 0.5 collective-permute-start.36
  221.1 1.0 collective-permute-done.39.refs_2_
  222.2 4.3 %collective-permute-start.46 = (bf16[48,256]{1,0:T(8,128)(2,1)S(1)}, bf16[48,256]{1,0:T(8,128)(2,1)S(1)}, u32[]{:S(2)}, u32[]{:S(2)}) collective-permute-start(bf16[48,256]{1,0:T(8,128)(2,1)S(1)} %get-tuple-element.165), channel_id=1, source_target_pairs={{0,1},{1,0},{2,3},{3,2},{4,5},{5,4},{6,7},{7,6},{8,9},{9,8},{10,11... | collective-permute-start | bytes 73736 | tf_op jit(solution)/shard_map/ppermute | solution.py:705
  226.5 0.7 collective-permute-start.43
  227.6 0.8 collective-permute-start.45
  228.5 0.8 collective-permute-start.40
  229.3 2.8 %collective-permute-start.41 = (bf16[192,256]{1,0:T(8,128)(2,1)S(1)}, bf16[192,256]{1,0:T(8,128)(2,1)S(1)}, u32[]{:S(2)}, u32[]{:S(2)}) collective-permute-start(bf16[192,256]{1,0:T(8,128)(2,1)S(1)} %fourth_kernel.3.refs_0_), channel_id=1, source_target_pairs={{0,1},{1,0},{2,3},{3,2},{4,5},{5,4},{6,7},{7,6},{8,9},{9,8},{10,11... | collective-permute-start | bytes 294920 | tf_op jit(solution)/shard_map/ppermute | solution.py:705
  232.1 0.7 collective-permute-start.42
  232.8 0.6 multiply_subtract_fusion
  233.6 2.5 %adam.2 = (f32[192,2048]{1,0:T(8,128)}, f32[192,2048]{1,0:T(8,128)}, f32[192,2048]{1,0:T(8,128)}) custom-call(bf16[192,256]{1,0:T(8,128)(2,1)S(1)} %get-tuple-element.154.refs_0_, bf16[192,256]{1,0:T(8,128)(2,1)S(1)} %collective-permute-done.43.refs_1_, bf16[192,256]{1,0:T(8,128)(2,1)S(1)} %collective-permute-done.44.refs_2_, ...), custom_call_target="tpu_custom_call" | custom-call | tf_op jit(solution)/shard_map/adam/pallas_call | solution.py:687
  236.2 1.2 collective-permute-done.42.refs_3_
  237.4 2.5 %adam.3 = (f32[192,2048]{1,0:T(8,128)}, f32[192,2048]{1,0:T(8,128)}, f32[192,2048]{1,0:T(8,128)}) custom-call(bf16[192,256]{1,0:T(8,128)(2,1)S(1)} %fourth_kernel.3.refs_0_, bf16[192,256]{1,0:T(8,128)(2,1)S(1)} %collective-permute-done.40.refs_1_, ...), custom_call_target="tpu_custom_call", output_to_operand_aliasing={{0}: (7, {}), {1}: (8, {}), {2}: (9, {})} | custom-call | tf_op jit(solution)/shard_map/adam/pallas_call | solution.py:687
  (149 shorter events, 8.7 us)
Async XLA Ops:
  1.7 10.4 %collective-permute-start = (bf16[192,256]{1,0:T(8,128)(2,1)S(1)}, bf16[192,256]{1,0:T(8,128)(2,1)S(1)}, u32[]{:S(2)}, u32[]{:S(2)}) collective-permute-start(bf16[192,256]{1,0:T(8,128)(2,1)S(1)} %get-tuple-element.170), channel_id=1, source_target_pairs={{0,8},{4,12},{8,16},{12,20},{16,24},{20,28},{24,0},{28,4},{1,9},{5... | collective-permute-start | bytes 294920 | tf_op jit(solution)/shard_map/ppermute | solution.py:710
  3.1 9.1 %collective-permute-start.1 = (bf16[192,256]{1,0:T(8,128)(2,1)S(1)}, bf16[192,256]{1,0:T(8,128)(2,1)S(1)}, u32[]{:S(2)}, u32[]{:S(2)}) collective-permute-start(bf16[192,256]{1,0:T(8,128)(2,1)S(1)} %get-tuple-element.170), channel_id=1, source_target_pairs={{0,16},{4,20},{8,24},{12,28},{16,0},{20,4},{24,8},{28,12},{1,17},{... | collective-permute-start | bytes 294920 | tf_op jit(solution)/shard_map/ppermute | solution.py:710
  3.1 9.0 %collective-permute-start.2 = (bf16[192,256]{1,0:T(8,128)(2,1)S(1)}, bf16[192,256]{1,0:T(8,128)(2,1)S(1)}, u32[]{:S(2)}, u32[]{:S(2)}) collective-permute-start(bf16[192,256]{1,0:T(8,128)(2,1)S(1)} %get-tuple-element.170), channel_id=1, source_target_pairs={{0,24},{4,28},{8,0},{12,4},{16,8},{20,12},{24,16},{28,20},{1,25},{... | collective-permute-start | bytes 294920 | tf_op jit(solution)/shard_map/ppermute | solution.py:710
  12.2 39.4 %copy-start.11 = (bf16[4,192,256]{2,1,0:T(8,128)(2,1)}, bf16[4,192,256]{2,1,0:T(8,128)(2,1)S(1)}, u32[]{:S(2)}) copy-start(bf16[4,192,256]{2,1,0:T(8,128)(2,1)S(1)} %pad_maximum_fusion.refs_0_) | copy-start | bytes 1179652
  12.2 9.4 %collective-permute-start.3 = (bf16[4,192,256]{2,1,0:T(8,128)(2,1)S(1)}, bf16[4,192,256]{2,1,0:T(8,128)(2,1)S(1)}, u32[]{:S(2)}, u32[]{:S(2)}) collective-permute-start(bf16[4,192,256]{2,1,0:T(8,128)(2,1)S(1)} %pad_maximum_fusion.refs_0_), channel_id=1, source_target_pairs={{0,4},{4,0},{8,12},{12,8},{16,20},{20,16},{24,28},{28,24},{1,5},{5... | collective-permute-start | bytes 1179656 | tf_op jit(solution)/shard_map/ppermute | solution.py:705
  13.5 8.9 %collective-permute-start.4 = (bf16[4,192,256]{2,1,0:T(8,128)(2,1)S(1)}, bf16[4,192,256]{2,1,0:T(8,128)(2,1)S(1)}, u32[]{:S(2)}, u32[]{:S(2)}) collective-permute-start(bf16[4,192,256]{2,1,0:T(8,128)(2,1)S(1)} %pad_maximum_fusion.refs_0_), channel_id=1, source_target_pairs={{0,2},{1,3},{2,0},{3,1},{4,6},{5,7},{6,4},{7,5},{8,10},{9,11},{10,... | collective-permute-start | bytes 1179656 | tf_op jit(solution)/shard_map/ppermute | solution.py:705
  14.7 7.8 %collective-permute-start.7 = (bf16[192,256]{1,0:T(8,128)(2,1)S(1)}, bf16[192,256]{1,0:T(8,128)(2,1)S(1)}, u32[]{:S(2)}, u32[]{:S(2)}) collective-permute-start(bf16[192,256]{1,0:T(8,128)(2,1)S(1)} %get-tuple-element.91), channel_id=1, source_target_pairs={{0,8},{4,12},{8,16},{12,20},{16,24},{20,28},{24,0},{28,4},{1,9},{5... | collective-permute-start | bytes 294920 | tf_op jit(solution)/shard_map/ppermute | solution.py:710
  15.3 8.5 %collective-permute-start.8 = (bf16[192,256]{1,0:T(8,128)(2,1)S(1)}, bf16[192,256]{1,0:T(8,128)(2,1)S(1)}, u32[]{:S(2)}, u32[]{:S(2)}) collective-permute-start(bf16[192,256]{1,0:T(8,128)(2,1)S(1)} %get-tuple-element.91), channel_id=1, source_target_pairs={{0,16},{4,20},{8,24},{12,28},{16,0},{20,4},{24,8},{28,12},{1,17},{... | collective-permute-start | bytes 294920 | tf_op jit(solution)/shard_map/ppermute | solution.py:710
  17.6 8.5 %collective-permute-start.9 = (bf16[192,256]{1,0:T(8,128)(2,1)S(1)}, bf16[192,256]{1,0:T(8,128)(2,1)S(1)}, u32[]{:S(2)}, u32[]{:S(2)}) collective-permute-start(bf16[192,256]{1,0:T(8,128)(2,1)S(1)} %get-tuple-element.91), channel_id=1, source_target_pairs={{0,24},{4,28},{8,0},{12,4},{16,8},{20,12},{24,16},{28,20},{1,25},{... | collective-permute-start | bytes 294920 | tf_op jit(solution)/shard_map/ppermute | solution.py:710
  21.7 29.9 %copy-start.15 = (bf16[4,192,256]{2,1,0:T(8,128)(2,1)}, bf16[4,192,256]{2,1,0:T(8,128)(2,1)S(1)}, u32[]{:S(2)}) copy-start(bf16[4,192,256]{2,1,0:T(8,128)(2,1)S(1)} %collective-permute-done.3.refs_1_) | copy-start | bytes 1179652
  22.5 29.2 %copy-start.16 = (bf16[4,192,256]{2,1,0:T(8,128)(2,1)}, bf16[4,192,256]{2,1,0:T(8,128)(2,1)S(1)}, u32[]{:S(2)}) copy-start(bf16[4,192,256]{2,1,0:T(8,128)(2,1)S(1)} %collective-permute-done.4.refs_2_) | copy-start | bytes 1179652
  26.2 25.5 %copy-start.12 = (bf16[4,192,256]{2,1,0:T(8,128)(2,1)}, bf16[4,192,256]{2,1,0:T(8,128)(2,1)S(1)}, u32[]{:S(2)}) copy-start(bf16[4,192,256]{2,1,0:T(8,128)(2,1)S(1)} %pad_maximum_fusion.1.refs_10_) | copy-start | bytes 1179652
  26.2 9.8 %collective-permute-start.10 = (bf16[4,192,256]{2,1,0:T(8,128)(2,1)S(1)}, bf16[4,192,256]{2,1,0:T(8,128)(2,1)S(1)}, u32[]{:S(2)}, u32[]{:S(2)}) collective-permute-start(bf16[4,192,256]{2,1,0:T(8,128)(2,1)S(1)} %pad_maximum_fusion.1.refs_10_), channel_id=1, source_target_pairs={{0,4},{4,0},{8,12},{12,8},{16,20},{20,16},{24,28},{28,24},{1,5},{5... | collective-permute-start | bytes 1179656 | tf_op jit(solution)/shard_map/ppermute | solution.py:705
  26.5 9.9 %collective-permute-start.11 = (bf16[4,192,256]{2,1,0:T(8,128)(2,1)S(1)}, bf16[4,192,256]{2,1,0:T(8,128)(2,1)S(1)}, u32[]{:S(2)}, u32[]{:S(2)}) collective-permute-start(bf16[4,192,256]{2,1,0:T(8,128)(2,1)S(1)} %pad_maximum_fusion.1.refs_10_), channel_id=1, source_target_pairs={{0,2},{1,3},{2,0},{3,1},{4,6},{5,7},{6,4},{7,5},{8,10},{9,11},{10,... | collective-permute-start | bytes 1179656 | tf_op jit(solution)/shard_map/ppermute | solution.py:705
  26.7 13.5 %collective-permute-start.5 = (bf16[4,192,128]{2,1,0:T(8,128)(2,1)S(1)}, bf16[4,192,128]{2,1,0:T(8,128)(2,1)S(1)}, u32[]{:S(2)}, u32[]{:S(2)}) collective-permute-start(bf16[4,192,128]{2,1,0:T(8,128)(2,1)S(1)} %slice.60), channel_id=1, source_target_pairs={{0,2},{1,3},{2,0},{3,1},{4,6},{5,7},{6,4},{7,5},{8,10},{9,11},{10,... | collective-permute-start | bytes 589832 | tf_op jit(solution)/shard_map/ppermute | solution.py:705
  28.0 12.3 %collective-permute-start.6 = (bf16[4,192,128]{2,1,0:T(8,128)(2,1)S(1)}, bf16[4,192,128]{2,1,0:T(8,128)(2,1)S(1)}, u32[]{:S(2)}, u32[]{:S(2)}) collective-permute-start(bf16[4,192,128]{2,1,0:T(8,128)(2,1)S(1)} %slice.61), channel_id=1, source_target_pairs={{0,4},{4,0},{8,12},{12,8},{16,20},{20,16},{24,28},{28,24},{1,5},{5... | collective-permute-start | bytes 589832 | tf_op jit(solution)/shard_map/ppermute | solution.py:705
  36.0 15.6 %copy-start.17 = (bf16[4,192,256]{2,1,0:T(8,128)(2,1)}, bf16[4,192,256]{2,1,0:T(8,128)(2,1)S(1)}, u32[]{:S(2)}) copy-start(bf16[4,192,256]{2,1,0:T(8,128)(2,1)S(1)} %collective-permute-done.10.refs_11_) | copy-start | bytes 1179652
  36.1 8.4 %collective-permute-start.17 = (bf16[4,192,128]{2,1,0:T(8,128)(2,1)S(1)}, bf16[4,192,128]{2,1,0:T(8,128)(2,1)S(1)}, u32[]{:S(2)}, u32[]{:S(2)}) collective-permute-start(bf16[4,192,128]{2,1,0:T(8,128)(2,1)S(1)} %slice.62), channel_id=1, source_target_pairs={{0,2},{1,3},{2,0},{3,1},{4,6},{5,7},{6,4},{7,5},{8,10},{9,11},{10,... | collective-permute-start | bytes 589832 | tf_op jit(solution)/shard_map/ppermute | solution.py:705
  36.3 15.3 %copy-start.18 = (bf16[4,192,256]{2,1,0:T(8,128)(2,1)}, bf16[4,192,256]{2,1,0:T(8,128)(2,1)S(1)}, u32[]{:S(2)}) copy-start(bf16[4,192,256]{2,1,0:T(8,128)(2,1)S(1)} %collective-permute-done.11.refs_12_) | copy-start | bytes 1179652
  36.4 8.1 %collective-permute-start.18 = (bf16[4,192,128]{2,1,0:T(8,128)(2,1)S(1)}, bf16[4,192,128]{2,1,0:T(8,128)(2,1)S(1)}, u32[]{:S(2)}, u32[]{:S(2)}) collective-permute-start(bf16[4,192,128]{2,1,0:T(8,128)(2,1)S(1)} %slice.63), channel_id=1, source_target_pairs={{0,4},{4,0},{8,12},{12,8},{16,20},{20,16},{24,28},{28,24},{1,5},{5... | collective-permute-start | bytes 589832 | tf_op jit(solution)/shard_map/ppermute | solution.py:705
  40.2 10.6 %copy-start.30 = (bf16[4,192,128]{2,1,0:T(8,128)(2,1)}, bf16[4,192,128]{2,1,0:T(8,128)(2,1)S(1)}, u32[]{:S(2)}) copy-start(bf16[4,192,128]{2,1,0:T(8,128)(2,1)S(1)} %collective-permute-done.5.refs_3_) | copy-start | bytes 589828
  40.2 10.6 %copy-start.31 = (bf16[4,192,128]{2,1,0:T(8,128)(2,1)}, bf16[4,192,128]{2,1,0:T(8,128)(2,1)S(1)}, u32[]{:S(2)}) copy-start(bf16[4,192,128]{2,1,0:T(8,128)(2,1)S(1)} %collective-permute-done.6.refs_4_) | copy-start | bytes 589828
  40.2 8.0 %collective-permute-start.12 = (bf16[4,192,256]{2,1,0:T(8,128)(2,1)S(1)}, bf16[4,192,256]{2,1,0:T(8,128)(2,1)S(1)}, u32[]{:S(2)}, u32[]{:S(2)}) collective-permute-start(bf16[4,192,256]{2,1,0:T(8,128)(2,1)S(1)} %pad_maximum_fusion.refs_0_), channel_id=1, source_target_pairs={{0,1},{1,0},{2,3},{3,2},{4,5},{5,4},{6,7},{7,6},{8,9},{9,8},{10,11... | collective-permute-start | bytes 1179656 | tf_op jit(solution)/shard_map/ppermute | solution.py:705
  44.0 2.6 %collective-permute-start.15 = (bf16[4,192,128]{2,1,0:T(8,128)(2,1)S(1)}, bf16[4,192,128]{2,1,0:T(8,128)(2,1)S(1)}, u32[]{:S(2)}, u32[]{:S(2)}) collective-permute-start(bf16[4,192,128]{2,1,0:T(8,128)(2,1)S(1)} %collective-permute-done.5.refs_3_), channel_id=1, source_target_pairs={{0,1},{1,0},{2,3},{3,2},{4,5},{5,4},{6,7},{7,6},{8,9},{9,8},{10,11... | collective-permute-start | bytes 589832 | tf_op jit(solution)/shard_map/ppermute | solution.py:705
  44.0 3.0 %collective-permute-start.16 = (bf16[4,192,128]{2,1,0:T(8,128)(2,1)S(1)}, bf16[4,192,128]{2,1,0:T(8,128)(2,1)S(1)}, u32[]{:S(2)}, u32[]{:S(2)}) collective-permute-start(bf16[4,192,128]{2,1,0:T(8,128)(2,1)S(1)} %collective-permute-done.6.refs_4_), channel_id=1, source_target_pairs={{0,1},{1,0},{2,3},{3,2},{4,5},{5,4},{6,7},{7,6},{8,9},{9,8},{10,11... | collective-permute-start | bytes 589832 | tf_op jit(solution)/shard_map/ppermute | solution.py:705
  44.5 6.3 %copy-start.32 = (bf16[4,192,128]{2,1,0:T(8,128)(2,1)}, bf16[4,192,128]{2,1,0:T(8,128)(2,1)S(1)}, u32[]{:S(2)}) copy-start(bf16[4,192,128]{2,1,0:T(8,128)(2,1)S(1)} %collective-permute-done.17.refs_13_) | copy-start | bytes 589828
  44.5 6.3 %copy-start.33 = (bf16[4,192,128]{2,1,0:T(8,128)(2,1)}, bf16[4,192,128]{2,1,0:T(8,128)(2,1)S(1)}, u32[]{:S(2)}) copy-start(bf16[4,192,128]{2,1,0:T(8,128)(2,1)S(1)} %collective-permute-done.18.refs_14_) | copy-start | bytes 589828
  44.5 3.1 %collective-permute-start.22 = (bf16[4,192,128]{2,1,0:T(8,128)(2,1)S(1)}, bf16[4,192,128]{2,1,0:T(8,128)(2,1)S(1)}, u32[]{:S(2)}, u32[]{:S(2)}) collective-permute-start(bf16[4,192,128]{2,1,0:T(8,128)(2,1)S(1)} %collective-permute-done.17.refs_13_), channel_id=1, source_target_pairs={{0,1},{1,0},{2,3},{3,2},{4,5},{5,4},{6,7},{7,6},{8,9},{9,8},{10,11... | collective-permute-start | bytes 589832 | tf_op jit(solution)/shard_map/ppermute | solution.py:705
  46.5 1.5 collective-permute-start.23
  46.6 2.0 collective-permute-start.13
  47.0 2.0 collective-permute-start.14
  47.6 2.1 collective-permute-start.19
  48.0 2.8 %collective-permute-start.20 = (bf16[4,192,256]{2,1,0:T(8,128)(2,1)S(1)}, bf16[4,192,256]{2,1,0:T(8,128)(2,1)S(1)}, u32[]{:S(2)}, u32[]{:S(2)}) collective-permute-start(bf16[4,192,256]{2,1,0:T(8,128)(2,1)S(1)} %collective-permute-done.10.refs_11_), channel_id=1, source_target_pairs={{0,1},{1,0},{2,3},{3,2},{4,5},{5,4},{6,7},{7,6},{8,9},{9,8},{10,11... | collective-permute-start | bytes 1179656 | tf_op jit(solution)/shard_map/ppermute | solution.py:705
  48.2 3.3 %collective-permute-start.21 = (bf16[4,192,256]{2,1,0:T(8,128)(2,1)S(1)}, bf16[4,192,256]{2,1,0:T(8,128)(2,1)}, u32[]{:S(2)}, u32[]{:S(2)}) collective-permute-start(bf16[4,192,256]{2,1,0:T(8,128)(2,1)S(1)} %collective-permute-done.11.refs_12_), channel_id=1, source_target_pairs={{0,1},{1,0},{2,3},{3,2},{4,5},{5,4},{6,7},{7,6},{8,9},{9,8},{10,11... | collective-permute-start | bytes 1179656 | tf_op jit(solution)/shard_map/ppermute | solution.py:705
  175.9 3.5 %collective-permute-start.27 = (bf16[1536,512]{1,0:T(8,128)(2,1)S(1)}, bf16[1536,512]{1,0:T(8,128)(2,1)S(1)}, u32[]{:S(2)}, u32[]{:S(2)}) collective-permute-start(bf16[1536,512]{1,0:T(8,128)(2,1)S(1)} %convolution_convert_fusion), channel_id=1, source_target_pairs={{0,1},{1,0},{2,3},{3,2},{4,5},{5,4},{6,7},{7,6},{8,9},{9,8},{10,11... | collective-permute-start | bytes 4718600 | tf_op jit(solution)/shard_map/ppermute | solution.py:705
  178.1 4.9 %collective-permute-start.24 = (bf16[1536,512]{1,0:T(8,128)(2,1)S(1)}, bf16[1536,512]{1,0:T(8,128)(2,1)S(1)}, u32[]{:S(2)}, u32[]{:S(2)}) collective-permute-start(bf16[1536,512]{1,0:T(8,128)(2,1)S(1)} %convolution_convert_fusion.1), channel_id=1, source_target_pairs={{0,1},{1,0},{2,3},{3,2},{4,5},{5,4},{6,7},{7,6},{8,9},{9,8},{10,11... | collective-permute-start | bytes 4718600 | tf_op jit(solution)/shard_map/ppermute | solution.py:705
  181.4 11.0 %collective-permute-start.28 = (bf16[1632,128]{1,0:T(8,128)(2,1)S(1)}, bf16[1632,128]{1,0:T(8,128)(2,1)S(1)}, u32[]{:S(2)}, u32[]{:S(2)}) collective-permute-start(bf16[1632,128]{1,0:T(8,128)(2,1)S(1)} %get-tuple-element.115), channel_id=1, source_target_pairs={{0,2},{1,3},{2,0},{3,1},{4,6},{5,7},{6,4},{7,5},{8,10},{9,11},{10,... | collective-permute-start | bytes 1253384 | tf_op jit(solution)/shard_map/ppermute | solution.py:705
  181.8 10.2 %collective-permute-start.29 = (bf16[4,192,256]{2,1,0:T(8,128)(2,1)S(1)}, bf16[4,192,256]{2,1,0:T(8,128)(2,1)S(1)}, u32[]{:S(2)}, u32[]{:S(2)}) collective-permute-start(bf16[4,192,256]{2,1,0:T(8,128)(2,1)S(1)} %get-tuple-element.116), channel_id=1, source_target_pairs={{0,4},{4,0},{8,12},{12,8},{16,20},{20,16},{24,28},{28,24},{1,5},{5... | collective-permute-start | bytes 1179656 | tf_op jit(solution)/shard_map/ppermute | solution.py:705
  185.0 15.8 %collective-permute-start.25 = (bf16[1536,128]{1,0:T(8,128)(2,1)S(1)}, bf16[1536,128]{1,0:T(8,128)(2,1)S(1)}, u32[]{:S(2)}, u32[]{:S(2)}) collective-permute-start(bf16[1536,128]{1,0:T(8,128)(2,1)S(1)} %get-tuple-element.112), channel_id=1, source_target_pairs={{0,2},{1,3},{2,0},{3,1},{4,6},{5,7},{6,4},{7,5},{8,10},{9,11},{10,... | collective-permute-start | bytes 1179656 | tf_op jit(solution)/shard_map/ppermute | solution.py:705
  186.2 14.6 %collective-permute-start.26 = (bf16[4,192,256]{2,1,0:T(8,128)(2,1)S(1)}, bf16[4,192,256]{2,1,0:T(8,128)(2,1)S(1)}, u32[]{:S(2)}, u32[]{:S(2)}) collective-permute-start(bf16[4,192,256]{2,1,0:T(8,128)(2,1)S(1)} %get-tuple-element.113), channel_id=1, source_target_pairs={{0,4},{4,0},{8,12},{12,8},{16,20},{20,16},{24,28},{28,24},{1,5},{5... | collective-permute-start | bytes 1179656 | tf_op jit(solution)/shard_map/ppermute | solution.py:705
  192.7 12.5 %collective-permute-start.32 = (bf16[864,128]{1,0:T(8,128)(2,1)S(1)}, bf16[864,128]{1,0:T(8,128)(2,1)S(1)}, u32[]{:S(2)}, u32[]{:S(2)}) collective-permute-start(bf16[864,128]{1,0:T(8,128)(2,1)S(1)} %get-tuple-element.117), channel_id=1, source_target_pairs={{0,4},{4,0},{8,12},{12,8},{16,20},{20,16},{24,28},{28,24},{1,5},{5... | collective-permute-start | bytes 663560 | tf_op jit(solution)/shard_map/ppermute | solution.py:705
  194.0 11.1 %collective-permute-start.33 = (bf16[4,192,128]{2,1,0:T(8,128)(2,1)S(1)}, bf16[4,192,128]{2,1,0:T(8,128)(2,1)S(1)}, u32[]{:S(2)}, u32[]{:S(2)}) collective-permute-start(bf16[4,192,128]{2,1,0:T(8,128)(2,1)S(1)} %get-tuple-element.118), channel_id=1, source_target_pairs={{0,2},{1,3},{2,0},{3,1},{4,6},{5,7},{6,4},{7,5},{8,10},{9,11},{10,... | collective-permute-start | bytes 589832 | tf_op jit(solution)/shard_map/ppermute | solution.py:705
  201.1 12.1 %copy-start.4 = (bf16[512,2048]{1,0:T(8,128)(2,1)S(1)}, bf16[512,2048]{1,0:T(8,128)(2,1)}, u32[]{:S(2)}) copy-start(bf16[512,2048]{1,0:T(8,128)(2,1)} %get-tuple-element.144) | copy-start | bytes 6291460
  201.1 8.2 %collective-permute-start.30 = (bf16[768,128]{1,0:T(8,128)(2,1)S(1)}, bf16[768,128]{1,0:T(8,128)(2,1)S(1)}, u32[]{:S(2)}, u32[]{:S(2)}) collective-permute-start(bf16[768,128]{1,0:T(8,128)(2,1)S(1)} %get-tuple-element.123), channel_id=1, source_target_pairs={{0,4},{4,0},{8,12},{12,8},{16,20},{20,16},{24,28},{28,24},{1,5},{5... | collective-permute-start | bytes 589832 | tf_op jit(solution)/shard_map/ppermute | solution.py:705
  202.4 7.0 %collective-permute-start.31 = (bf16[4,192,128]{2,1,0:T(8,128)(2,1)S(1)}, bf16[4,192,128]{2,1,0:T(8,128)(2,1)S(1)}, u32[]{:S(2)}, u32[]{:S(2)}) collective-permute-start(bf16[4,192,128]{2,1,0:T(8,128)(2,1)S(1)} %get-tuple-element.124), channel_id=1, source_target_pairs={{0,2},{1,3},{2,0},{3,1},{4,6},{5,7},{6,4},{7,5},{8,10},{9,11},{10,... | collective-permute-start | bytes 589832 | tf_op jit(solution)/shard_map/ppermute | solution.py:705
  205.3 15.9 %collective-permute-start.37 = (bf16[240,256]{1,0:T(8,128)(2,1)S(1)}, bf16[240,256]{1,0:T(8,128)(2,1)S(1)}, u32[]{:S(2)}, u32[]{:S(2)}) collective-permute-start(bf16[240,256]{1,0:T(8,128)(2,1)S(1)} %get-tuple-element.130), channel_id=1, source_target_pairs={{0,8},{4,12},{8,16},{12,20},{16,24},{20,28},{24,0},{28,4},{1,9},{5... | collective-permute-start | bytes 368648 | tf_op jit(solution)/shard_map/ppermute | solution.py:710
  207.2 13.9 %collective-permute-start.38 = (bf16[240,256]{1,0:T(8,128)(2,1)S(1)}, bf16[240,256]{1,0:T(8,128)(2,1)S(1)}, u32[]{:S(2)}, u32[]{:S(2)}) collective-permute-start(bf16[240,256]{1,0:T(8,128)(2,1)S(1)} %get-tuple-element.131), channel_id=1, source_target_pairs={{0,16},{4,20},{8,24},{12,28},{16,0},{20,4},{24,8},{28,12},{1,17},{... | collective-permute-start | bytes 368648 | tf_op jit(solution)/shard_map/ppermute | solution.py:710
  208.7 13.4 %collective-permute-start.39 = (bf16[240,256]{1,0:T(8,128)(2,1)S(1)}, bf16[240,256]{1,0:T(8,128)(2,1)S(1)}, u32[]{:S(2)}, u32[]{:S(2)}) collective-permute-start(bf16[240,256]{1,0:T(8,128)(2,1)S(1)} %get-tuple-element.132), channel_id=1, source_target_pairs={{0,24},{4,28},{8,0},{12,4},{16,8},{20,12},{24,16},{28,20},{1,25},{... | collective-permute-start | bytes 368648 | tf_op jit(solution)/shard_map/ppermute | solution.py:710
  209.5 11.2 %collective-permute-start.34 = (bf16[192,256]{1,0:T(8,128)(2,1)S(1)}, bf16[192,256]{1,0:T(8,128)(2,1)S(1)}, u32[]{:S(2)}, u32[]{:S(2)}) collective-permute-start(bf16[192,256]{1,0:T(8,128)(2,1)S(1)} %get-tuple-element.137), channel_id=1, source_target_pairs={{0,8},{4,12},{8,16},{12,20},{16,24},{20,28},{24,0},{28,4},{1,9},{5... | collective-permute-start | bytes 294920 | tf_op jit(solution)/shard_map/ppermute | solution.py:710
  211.7 16.0 %collective-permute-start.35 = (bf16[192,256]{1,0:T(8,128)(2,1)S(1)}, bf16[192,256]{1,0:T(8,128)(2,1)S(1)}, u32[]{:S(2)}, u32[]{:S(2)}) collective-permute-start(bf16[192,256]{1,0:T(8,128)(2,1)S(1)} %get-tuple-element.138), channel_id=1, source_target_pairs={{0,16},{4,20},{8,24},{12,28},{16,0},{20,4},{24,8},{28,12},{1,17},{... | collective-permute-start | bytes 294920 | tf_op jit(solution)/shard_map/ppermute | solution.py:710
  216.8 16.9 %copy-start.2 = (f32[192,2048]{1,0:T(8,128)S(1)}, f32[192,2048]{1,0:T(8,128)}, u32[]{:S(2)}) copy-start(f32[192,2048]{1,0:T(8,128)} %refs_6_.3) | copy-start | bytes 4718596
  219.3 13.5 %copy-start.14 = (f32[5632]{0:T(1024)S(1)}, f32[5632]{0:T(1024)}, u32[]{:S(2)}) copy-start(f32[5632]{0:T(1024)} %param.23) | copy-start | bytes 67588
  219.3 13.5 %copy-start.21 = (f32[5632]{0:T(1024)S(1)}, f32[5632]{0:T(1024)}, u32[]{:S(2)}) copy-start(f32[5632]{0:T(1024)} %param.24) | copy-start | bytes 67588
  219.3 13.5 %copy-start.22 = (f32[5632]{0:T(1024)S(1)}, f32[5632]{0:T(1024)}, u32[]{:S(2)}) copy-start(f32[5632]{0:T(1024)} %param.25) | copy-start | bytes 67588
  219.3 14.3 %copy-start = (f32[192,2048]{1,0:T(8,128)S(1)}, f32[192,2048]{1,0:T(8,128)}, u32[]{:S(2)}) copy-start(f32[192,2048]{1,0:T(8,128)} %refs_4_.3) | copy-start | bytes 4718596
  219.3 14.3 %copy-start.1 = (f32[192,2048]{1,0:T(8,128)S(1)}, f32[192,2048]{1,0:T(8,128)}, u32[]{:S(2)}) copy-start(f32[192,2048]{1,0:T(8,128)} %refs_5_.3) | copy-start | bytes 4718596
  220.7 7.7 %collective-permute-start.36 = (bf16[192,256]{1,0:T(8,128)(2,1)S(1)}, bf16[192,256]{1,0:T(8,128)(2,1)S(1)}, u32[]{:S(2)}, u32[]{:S(2)}) collective-permute-start(bf16[192,256]{1,0:T(8,128)(2,1)S(1)} %get-tuple-element.139), channel_id=1, source_target_pairs={{0,24},{4,28},{8,0},{12,4},{16,8},{20,12},{24,16},{28,20},{1,25},{... | collective-permute-start | bytes 294920 | tf_op jit(solution)/shard_map/ppermute | solution.py:710
  222.2 7.1 %collective-permute-start.46 = (bf16[48,256]{1,0:T(8,128)(2,1)S(1)}, bf16[48,256]{1,0:T(8,128)(2,1)S(1)}, u32[]{:S(2)}, u32[]{:S(2)}) collective-permute-start(bf16[48,256]{1,0:T(8,128)(2,1)S(1)} %get-tuple-element.165), channel_id=1, source_target_pairs={{0,1},{1,0},{2,3},{3,2},{4,5},{5,4},{6,7},{7,6},{8,9},{9,8},{10,11... | collective-permute-start | bytes 73736 | tf_op jit(solution)/shard_map/ppermute | solution.py:705
  226.5 5.6 %collective-permute-start.43 = (bf16[192,256]{1,0:T(8,128)(2,1)S(1)}, bf16[192,256]{1,0:T(8,128)(2,1)S(1)}, u32[]{:S(2)}, u32[]{:S(2)}) collective-permute-start(bf16[192,256]{1,0:T(8,128)(2,1)S(1)} %get-tuple-element.154.refs_0_), channel_id=1, source_target_pairs={{0,2},{1,3},{2,0},{3,1},{4,6},{5,7},{6,4},{7,5},{8,10},{9,11},{10,... | collective-permute-start | bytes 294920 | tf_op jit(solution)/shard_map/ppermute | solution.py:705
  227.3 6.2 %collective-permute-start.44 = (bf16[192,256]{1,0:T(8,128)(2,1)S(1)}, bf16[192,256]{1,0:T(8,128)(2,1)S(1)}, u32[]{:S(2)}, u32[]{:S(2)}) collective-permute-start(bf16[192,256]{1,0:T(8,128)(2,1)S(1)} %get-tuple-element.154.refs_0_), channel_id=1, source_target_pairs={{0,1},{1,0},{2,3},{3,2},{4,5},{5,4},{6,7},{7,6},{8,9},{9,8},{10,11... | collective-permute-start | bytes 294920 | tf_op jit(solution)/shard_map/ppermute | solution.py:705
  227.6 6.0 %collective-permute-start.45 = (bf16[192,256]{1,0:T(8,128)(2,1)S(1)}, bf16[192,256]{1,0:T(8,128)(2,1)S(1)}, u32[]{:S(2)}, u32[]{:S(2)}) collective-permute-start(bf16[192,256]{1,0:T(8,128)(2,1)S(1)} %get-tuple-element.154.refs_0_), channel_id=1, source_target_pairs={{0,3},{1,2},{2,1},{3,0},{4,7},{5,6},{6,5},{7,4},{8,11},{9,10},{10,... | collective-permute-start | bytes 294920 | tf_op jit(solution)/shard_map/ppermute | solution.py:705
  228.5 7.7 %collective-permute-start.40 = (bf16[192,256]{1,0:T(8,128)(2,1)S(1)}, bf16[192,256]{1,0:T(8,128)(2,1)S(1)}, u32[]{:S(2)}, u32[]{:S(2)}) collective-permute-start(bf16[192,256]{1,0:T(8,128)(2,1)S(1)} %fourth_kernel.3.refs_0_), channel_id=1, source_target_pairs={{0,2},{1,3},{2,0},{3,1},{4,6},{5,7},{6,4},{7,5},{8,10},{9,11},{10,... | collective-permute-start | bytes 294920 | tf_op jit(solution)/shard_map/ppermute | solution.py:705
  229.3 6.9 %collective-permute-start.41 = (bf16[192,256]{1,0:T(8,128)(2,1)S(1)}, bf16[192,256]{1,0:T(8,128)(2,1)S(1)}, u32[]{:S(2)}, u32[]{:S(2)}) collective-permute-start(bf16[192,256]{1,0:T(8,128)(2,1)S(1)} %fourth_kernel.3.refs_0_), channel_id=1, source_target_pairs={{0,1},{1,0},{2,3},{3,2},{4,5},{5,4},{6,7},{7,6},{8,9},{9,8},{10,11... | collective-permute-start | bytes 294920 | tf_op jit(solution)/shard_map/ppermute | solution.py:705
  232.1 5.3 %collective-permute-start.42 = (bf16[192,256]{1,0:T(8,128)(2,1)S(1)}, bf16[192,256]{1,0:T(8,128)(2,1)S(1)}, u32[]{:S(2)}, u32[]{:S(2)}) collective-permute-start(bf16[192,256]{1,0:T(8,128)(2,1)S(1)} %fourth_kernel.3.refs_0_), channel_id=1, source_target_pairs={{0,3},{1,2},{2,1},{3,0},{4,7},{5,6},{6,5},{7,4},{8,11},{9,10},{10,... | collective-permute-start | bytes 294920 | tf_op jit(solution)/shard_map/ppermute | solution.py:705
  (23 other events, 52.8 us)
